TPU v7x, 128 devices: a whole 4x4x4 slice. The times are simulated.
128 devices in a mesh: blk: 16 (over x, y_hi, core), sub: 8 (over z, y_lo).
Axes of the slice: x: 4, y: 4 (y_hi: 2, y_lo: 2; y = y_hi * 2 + y_lo), z: 4, core: 2. Of those that a mesh axis runs over, the one named last changes fastest.
Arguments:
- left_emb: float32 [2, 200, 65536], P(None, None, ('blk', 'sub')), may hold values from -1.8 to 1.8
- left_state: float32 [65536], P(('blk', 'sub')), may hold values from 0.003 to 0.1
- right_emb: float32 [2, 200, 65536], P(None, None, ('blk', 'sub')), may hold values from -1.8 to 1.8
- right_state: float32 [65536], P(('blk', 'sub')), may hold values from 0.003 to 0.1
- relation_emb: float32 [2, 200, 1280], replicated, may hold values from -4.2 to 4.2
- relation_state: float32 [1280], replicated, may hold values from 0.003 to 0.1
- hub_emb: float32 [2, 200, 4096], replicated, may hold values from -1.8 to 1.8
- hub_state: float32 [4096], replicated, may hold values from 0.003 to 0.1
- heads: int32 [2, 65536], P(None, ('blk', 'sub')), may hold values from 0 to 511
- relations: int32 [2, 65536], P(None, ('blk', 'sub')), may hold values from 0 to 1279
- tails: int32 [2, 65536], P(None, ('blk', 'sub')), may hold values from 0 to 511
- negatives: int32 [2, 131072], P(None, ('blk', 'sub')), may hold values from 0 to 511
- hub_ids: int32 [2, 32768], P(None, ('blk', 'sub')), may hold values from 0 to 4095
Outputs:
- left_out: float32 [2, 200, 65536], P(None, None, ('blk', 'sub'))
- right_out: float32 [2, 200, 65536], P(None, None, ('blk', 'sub'))
- relation_out: float32 [2, 200, 1280], replicated
- hub_out: float32 [2, 200, 4096], replicated
Inputs may be any that keep to these rules, and one draw needn't show every extreme that they name: `heads`: local row indices of the head-side block. `relations`: relation types. `tails`: local row indices of the tail-side block held in that bucket. `negatives`: local row indices of the tail-side block held in that bucket; indices may repeat. `hub_ids`: hub rows; indices may repeat.
All inputs are finite; a program needn't handle non-finite values.
Results may differ from a plain program's by a relative error of at most 0.0001.
Values sent between devices are 32-bit elements; how exact they have to be, the bound alone decides.
A program may use at most 128 MiB of HBM per device.

v0:
```python
import functools
import jax
import jax.numpy as jnp
from jax import lax
from jax.experimental import pallas as pl
from jax.experimental.pallas import tpu as pltpu
from jax.sharding import PartitionSpec as P

RATE = 0.25
F32, BF16 = jnp.float32, jnp.bfloat16
NN = (((1,), (0,)), ((), ()))
NT = (((1,), (1,)), ((), ()))


def mm(a, b, dims=NN):
    return lax.dot_general(a, b, dims, preferred_element_type=F32)


def halves(x):
    hi = x.astype(BF16)
    return hi, (x - hi.astype(F32)).astype(BF16)


def stacked(x):
    hi, lo = halves(x)
    return jnp.concatenate([hi, lo], axis=0)


def mm3(a2, b_hi, b_lo, dims=NN):
    n = a2.shape[0] // 2
    both = mm(a2, b_hi, dims)
    return both[:n] + both[n:] + mm(a2[:n], b_lo, dims)


def fold(x):
    n = x.shape[0] // 2
    return x[:n] + x[n:]


def rows_hot(idx, base, count):
    at = lax.broadcasted_iota(jnp.int32, (count, idx.shape[1]), 0) + base
    return (at == idx).astype(F32).astype(BF16)


def column(idx):
    parts = []
    for k in range(0, idx.shape[1], 128):
        parts.append(jnp.broadcast_to(idx[:, k : k + 128], (128, 128)).T)
    return jnp.concatenate(parts, axis=0)


def lanes_hot(col, base, count):
    at = lax.broadcasted_iota(jnp.int32, (col.shape[0], 128), 1)
    return jnp.concatenate([col == at + (base + k) for k in range(0, count, 128)], axis=1)


def adagrad(table, state, grad):
    new_state = state + jnp.sum(grad * grad, axis=0, keepdims=True) * (1.0 / grad.shape[0])
    return table - grad * (RATE / jnp.sqrt(new_state)), new_state


def sigmoid(x):
    return 1.0 / (1.0 + jnp.exp(-x))


def cmul(a, b):
    n = a.shape[0] // 2
    a0, a1, b0, b1 = a[:n], a[n:], b[:n], b[n:]
    return jnp.concatenate([a0 * b0 - a1 * b1, a0 * b1 + a1 * b0], axis=0)


def cmul_conj(a, b):
    n = a.shape[0] // 2
    a0, a1, b0, b1 = a[:n], a[n:], b[:n], b[n:]
    return jnp.concatenate([a0 * b0 + a1 * b1, a1 * b0 - a0 * b1], axis=0)


def gather_loop(table_ref, idx, out_ref, block):
    count = table_ref.shape[1]
    out_ref[...] = jnp.zeros_like(out_ref)

    @pl.loop(0, count // block)
    def _(k):
        base = pl.multiple_of(k * block, block)
        out_ref[...] += mm(stacked(table_ref[:, pl.ds(base, block)]), rows_hot(idx, base, block))


def gather(table, idx):
    return mm(stacked(table), rows_hot(idx, 0, table.shape[1]))


def queries_side(q):
    qt = q.T
    return stacked(qt)


def first(bucket_weight, left_ref, lstate_ref, right_ref, rstate_ref, rel_ref, hub_ref, heads_ref, rels_ref,
          tails_ref, negs_ref, hubs_ref, left_out, lstate_out, right_out, rstate_out, h1_out, r1_out, q1_out,
          dqh1_out, dr0_out, ghub_out, u_ref, r_ref, du_ref):
    w = bucket_weight
    rows = left_ref.shape[1]
    e = heads_ref.shape[1]
    left = left_ref[...]
    right = right_ref[...]
    idx_r = jnp.concatenate([rels_ref[0:1, :], rels_ref[1:2, :]], axis=1)
    gather_loop(rel_ref, idx_r, r_ref, 256)
    h0 = fold(gather(left, heads_ref[0:1, :]))
    r0 = fold(r_ref[:, :e])
    q0 = cmul(h0, r0)
    q0t = stacked(q0.T)
    rh, rl = halves(right)
    coef = coefs(mm3(q0t, rh, rl), w, tails_ref[0:1, :], negs_ref[0:1, :], rows)
    ch, cl = halves(coef)
    q02 = stacked(q0)
    g = mm3(q02, ch, cl)
    right_out[...], rstate_out[...] = adagrad(right, rstate_ref[...], g)
    idx_u = jnp.concatenate([hubs_ref[0:1, :], hubs_ref[1:2, :]], axis=1)
    gather_loop(hub_ref, idx_u, u_ref, 512)
    m = hubs_ref.shape[1]
    u0h, u0l = u_ref[:400, :m].astype(BF16), u_ref[400:, :m].astype(BF16)
    ch2, cl2 = halves(sigmoid(mm3(q0t, u0h, u0l)) * w)
    du_ref[:, :m] = mm3(q02, ch2, cl2)
    r2 = jnp.concatenate([rh, rl], axis=0)
    u2 = jnp.concatenate([u0h, u0l], axis=0)
    dq = mm3(r2, ch, cl, NT) + mm3(u2, ch2, cl2, NT)
    dh = cmul_conj(dq, r0)
    dr0_out[...] = cmul_conj(dq, h0)
    gl = fold(mm(stacked(dh), lanes_hot(column(heads_ref[0:1, :]), 0, rows).astype(F32).astype(BF16)))
    left1, lstate_out[...] = adagrad(left, lstate_ref[...], gl)
    left_out[...] = left1
    h1 = fold(gather(left1, heads_ref[1:2, :]))
    r1 = fold(r_ref[:, e:])
    q1 = cmul(h1, r1)
    h1_out[...] = h1
    r1_out[...] = r1
    q1_out[...] = q1
    q1t = stacked(q1.T)
    u1h, u1l = u_ref[:400, m:].astype(BF16), u_ref[400:, m:].astype(BF16)
    ch3, cl3 = halves(sigmoid(mm3(q1t, u1h, u1l)) * w)
    du_ref[:, m:] = mm3(stacked(q1), ch3, cl3)
    dqh1_out[...] = mm3(jnp.concatenate([u1h, u1l], axis=0), ch3, cl3, NT)
    scatter_loop(du_ref[...], column(idx_u), ghub_out, 512)


def scatter_loop(grad, col, out_ref, block):
    g2 = stacked(grad)

    @pl.loop(0, out_ref.shape[1] // block)
    def _(k):
        base = pl.multiple_of(k * block, block)
        hot = lanes_hot(col, base, block).astype(F32).astype(BF16)
        out_ref[:, pl.ds(base, block)] = fold(mm(g2, hot))


def coefs(score, w, tail_idx, neg_idx, rows):
    times = jnp.sum(rows_hot_f(neg_idx, rows), axis=1, keepdims=True)
    times = jnp.broadcast_to(times, (rows, 128)).T[0:1, :] * w
    tail = lanes_hot(column(tail_idx), 0, rows)
    s = sigmoid(score)
    return s * times + jnp.where(tail, s - 1.0, 0.0)


def rows_hot_f(idx, count):
    at = lax.broadcasted_iota(jnp.int32, (count, idx.shape[1]), 0)
    return (at == idx).astype(F32)


def second(bucket_weight, left_ref, lstate_ref, right_ref, rstate_ref, h1_ref, r1_ref, q1_ref, dqh1_ref, dr0_ref,
           heads_ref, rels_ref, tails_ref, negs_ref, left_out, right_out, grel_out):
    w = bucket_weight
    right = right_ref[...]
    rows = right.shape[1]
    q1 = q1_ref[...]
    rh, rl = halves(right)
    coef = coefs(mm3(stacked(q1.T), rh, rl), w, tails_ref[1:2, :], negs_ref[1:2, :], rows)
    ch, cl = halves(coef)
    dq = mm3(jnp.concatenate([rh, rl], axis=0), ch, cl, NT) + dqh1_ref[...]
    dr = jnp.concatenate([dr0_ref[...], cmul_conj(dq, h1_ref[...])], axis=1)
    col_r = column(jnp.concatenate([rels_ref[0:1, :], rels_ref[1:2, :]], axis=1))
    scatter_loop(dr, col_r, grel_out, 256)
    dh = cmul_conj(dq, r1_ref[...])
    g = mm3(stacked(q1), ch, cl)
    right_out[...], _ = adagrad(right, rstate_ref[...], g)
    gl = fold(mm(stacked(dh), lanes_hot(column(heads_ref[1:2, :]), 0, rows).astype(F32).astype(BF16)))
    left_out[...], _ = adagrad(left_ref[...], lstate_ref[...], gl)


def shards(left_emb, left_state, right_emb, right_state, relation_emb, relation_state, hub_emb, hub_state, heads,
           relations, tails, negatives, hub_ids):
    two, half, rows = left_emb.shape
    feats = two * half
    e = heads.shape[1]
    w = 1.0 / (negatives.shape[1] + hub_ids.shape[1])
    left = left_emb.reshape(feats, rows)
    right = right_emb.reshape(feats, rows)
    rel = relation_emb.reshape(feats, -1)
    hub = hub_emb.reshape(feats, -1)
    sd = lambda *s: jax.ShapeDtypeStruct(s, F32)
    vm = pl.BlockSpec(memory_space=pltpu.VMEM)
    params = pltpu.CompilerParams(vmem_limit_bytes=56 * 2**20)
    outs = [sd(feats, rows), sd(1, rows), sd(feats, rows), sd(1, rows), sd(feats, e), sd(feats, e), sd(feats, e),
            sd(feats, e), sd(feats, e), sd(feats, hub.shape[1])]
    left1, ls1, right1, rs1, h1, r1, q1, dqh1, dr0, ghub = pl.pallas_call(
        functools.partial(first, w), out_shape=outs, in_specs=[vm] * 11, out_specs=[vm] * len(outs),
        scratch_shapes=[pltpu.VMEM((2 * feats, 2 * hub_ids.shape[1]), F32), pltpu.VMEM((2 * feats, 2 * e), F32),
                        pltpu.VMEM((feats, 2 * hub_ids.shape[1]), F32)],
        compiler_params=params, name="first_bucket",
    )(left, left_state[None], right, right_state[None], rel, hub, heads, relations, tails, negatives, hub_ids)
    n = lax.axis_size("blk")
    right1, rs1 = lax.ppermute((right1, rs1), "blk", [(i, (i + 1) % n) for i in range(n)])
    outs = [sd(feats, rows), sd(feats, rows), sd(feats, rel.shape[1])]
    left2, right2, grel = pl.pallas_call(
        functools.partial(second, w), out_shape=outs, in_specs=[vm] * 13, out_specs=[vm] * 3,
        compiler_params=params, name="second_bucket",
    )(left1, ls1, right1, rs1, h1, r1, q1, dqh1, dr0, heads, relations, tails, negatives)
    grel, ghub = lax.psum((grel, ghub), ("blk", "sub"))

    def step(table, state, grads):
        new = state + jnp.mean(grads * grads, axis=0)
        return table - RATE * grads / jnp.sqrt(new)[None, :]

    return (left2.reshape(left_emb.shape), right2.reshape(right_emb.shape),
            step(rel, relation_state, grel).reshape(relation_emb.shape),
            step(hub, hub_state, ghub).reshape(hub_emb.shape))


def solution(mesh):
    cut = P(None, None, ("blk", "sub"))
    row = P(("blk", "sub"))
    idx = P(None, ("blk", "sub"))
    return jax.shard_map(shards, mesh=mesh, in_specs=(cut, row, cut, row, P(), P(), P(), P(), idx, idx, idx, idx, idx),
                         out_specs=(cut, cut, P(), P()), check_vma=False)
```

profile of v0, /device:TPU:1, one launch (start us, length us, event | category | flops | bytes accessed | tf_op | source)
XLA Modules:
  0.0 245.8 jit_solution(7242091837024278610)
XLA Ops:
  7.2 0.0 all-reduce.3.cloned.1.call-start
  7.2 30.1 %first_bucket.1 = (f32[400,512]{1,0:T(8,128)}, f32[1,512]{1,0:T(1,128)}, f32[400,512]{1,0:T(8,128)}, f32[1,512]{1,0:T(1,128)}, f32[400,512]{1,0:T(8,128)}, /*ind...) custom-call(f32[400,512]{1,0:T(8,128)} %bitcast.18, ...), custom_call_target="tpu_custom_call" | custom-call | tf_op jit(solution)/shard_map/first_bucket/pallas_call | solution.py:203
  37.4 4.3 %collective-permute-start = (f32[400,512]{1,0:T(8,128)}, f32[400,512]{1,0:T(8,128)S(1)}, u32[]{:S(2)}, u32[]{:S(2)}) collective-permute-start(f32[400,512]{1,0:T(8,128)} %get-tuple-element.19), channel_id=1, source_target_pairs={{0,8},{8,16},{16,24},{24,32},{32,40},{40,48},{48,56},{56,64},{64,7... | collective-permute-start | bytes 2457608 | tf_op jit(solution)/shard_map/ppermute | solution.py:210
  41.7 0.3 collective-permute-start.1
  41.9 9.3 %collective-permute-done.1.rstate_ref = f32[1,512]{1,0:T(1,128)S(1)} collective-permute-done((f32[1,512]{1,0:T(1,128)}, f32[1,512]{1,0:T(1,128)S(1)}, u32[]{:S(2)}, u32[]{:S(2)}) %collective-permute-start.1) | collective-permute-done | bytes 2080 | tf_op jit(solution)/shard_map/ppermute | solution.py:210
  51.3 0.0 copy-start.5
  51.3 0.0 collective-permute-done.right_ref
  51.3 0.0 copy-start.2
  51.3 0.6 copy-done.5
  51.8 0.4 copy-done.2
  52.2 10.6 %second_bucket.1 = (f32[400,512]{1,0:T(8,128)}, f32[400,512]{1,0:T(8,128)}, f32[400,1280]{1,0:T(8,128)}) custom-call(f32[400,512]{1,0:T(8,128)} %get-tuple-element.17.left_ref, f32[1,512]{1,0:T(1,128)} %get-tuple-element.18.lstate_ref, f32[400,512]{1,0:T(8,128)} %copy-done.2, f32[1,512]{1,0:T(1,128)} %copy-done.5, f32[400,512]{1,0:T(8,128)} %get-tuple-element.21.h1_ref, ...), custom_call_target="tpu_custom_call" | custom-call | tf_op jit(solution)/shard_map/second_bucket/pallas_call | solution.py:212
  62.8 0.0 copy-start.4
  62.8 0.0 copy-start.1
  62.8 0.0 all-reduce.3.cloned.1.call-update
  62.9 165.2 %all-reduce.3.cloned.1.call-done = (f32[400,1280]{1,0:T(8,128)}, f32[400,4096]{1,0:T(8,128)}) async-done(((f32[400,1280]{1,0:T(8,128)}, f32[400,4096]{1,0:T(8,128)}), (f32[400,1280]{1,0:T(8,128)}, f32[400,4096]{1,0:T(8,128)})) %all-reduce.3.cloned.1.call-update) | async-done | bytes 8601616 | tf_op jit(solution)/shard_map/psum | solution.py:216
  228.0 0.0 copy-start
  228.0 0.0 slice-start
  228.0 1.9 multiply_reduce_fusion.1
  229.9 0.0 copy-done.4
  229.9 0.0 copy-start.3
  229.9 0.0 copy-done.1
  230.0 0.0 slice-start.1
  230.0 3.9 %divide_subtract_fusion.1 = f32[400,1280]{1,0:T(8,128)} fusion(f32[400,1280]{1,0:T(8,128)} %get-tuple-element.30, f32[1280]{0:T(1024)S(1)} %add_sqrt_fusion.1, f32[2,200,1280]{2,1,0:T(8,128)S(1)} %copy-done.1), kind=kLoop, calls=%fused_computation.2 | loop fusion | flops 1536000 | bytes 6149120 | tf_op jit(solution)/shard_map/sub | solution.py:220
  233.9 0.0 copy-done
  233.9 0.7 multiply_reduce_fusion
  234.5 0.0 copy-done.3
  234.6 0.0 slice-done
  234.6 0.4 slice-done.1
  235.0 4.0 %divide_subtract_fusion = f32[400,4096]{1,0:T(8,128)} fusion(f32[400,4096]{1,0:T(8,128)S(1)} %copy-done, f32[4096]{0:T(1024)S(1)} %add_sqrt_fusion, f32[2,200,4096]{2,1,0:T(8,128)S(1)} %bitcast.14), kind=kLoop, calls=%fused_computation | loop fusion | flops 4915200 | bytes 19677184 | tf_op jit(solution)/shard_map/sub | solution.py:220
  (3 shorter events, 0.0 us)
Async XLA Ops:
  7.2 220.8 %all-reduce.3.cloned.1.call-start = ((), (), s32[]{:S(2)}) async-start(), calls=%async_computation | async-start | bytes 17203200 | tf_op jit(solution)/shard_map/psum | solution.py:216
  37.4 13.9 %collective-permute-start = (f32[400,512]{1,0:T(8,128)}, f32[400,512]{1,0:T(8,128)S(1)}, u32[]{:S(2)}, u32[]{:S(2)}) collective-permute-start(f32[400,512]{1,0:T(8,128)} %get-tuple-element.19), channel_id=1, source_target_pairs={{0,8},{8,16},{16,24},{24,32},{32,40},{40,48},{48,56},{56,64},{64,7... | collective-permute-start | bytes 2457608 | tf_op jit(solution)/shard_map/ppermute | solution.py:210
  41.7 9.6 %collective-permute-start.1 = (f32[1,512]{1,0:T(1,128)}, f32[1,512]{1,0:T(1,128)S(1)}, u32[]{:S(2)}, u32[]{:S(2)}) collective-permute-start(f32[1,512]{1,0:T(1,128)} %get-tuple-element.20), channel_id=1, source_target_pairs={{0,8},{8,16},{16,24},{24,32},{32,40},{40,48},{48,56},{56,64},{64,7... | collective-permute-start | bytes 6152 | tf_op jit(solution)/shard_map/ppermute | solution.py:210
  51.3 0.6 copy-start.5
  51.3 0.9 copy-start.2
  62.8 167.1 %copy-start.4 = (f32[1280]{0:T(1024)S(1)}, f32[1280]{0:T(1024)}, u32[]{:S(2)}) copy-start(f32[1280]{0:T(1024)} %param.18) | copy-start | bytes 15364
  62.8 167.1 %copy-start.1 = (f32[2,200,1280]{2,1,0:T(8,128)S(1)}, f32[2,200,1280]{2,1,0:T(8,128)}, u32[]{:S(2)}) copy-start(f32[2,200,1280]{2,1,0:T(8,128)} %param.17) | copy-start | bytes 6144004
  228.0 5.9 %copy-start = (f32[400,4096]{1,0:T(8,128)S(1)}, f32[400,4096]{1,0:T(8,128)}, u32[]{:S(2)}) copy-start(f32[400,4096]{1,0:T(8,128)} %get-tuple-element.31) | copy-start | bytes 19660804
  228.0 6.6 %slice-start = ((s8[6553600]{0:T(1024)(128)(4,1)}), s8[4194304]{0:T(1024)(128)(4,1)S(1)}, s32[]{:S(2)}) async-start(s8[6553600]{0:T(1024)(128)(4,1)} %bitcast.13), calls=%async_computation.1 | async-start | bytes 8388608
  229.9 4.6 %copy-start.3 = (f32[4096]{0:T(1024)S(1)}, f32[4096]{0:T(1024)}, u32[]{:S(2)}) copy-start(f32[4096]{0:T(1024)} %param.20) | copy-start | bytes 49156
  230.0 5.0 %slice-start.1 = ((s8[6553600]{0:T(1024)(128)(4,1)}), s8[2359296]{0:T(1024)(128)(4,1)S(1)}, s32[]{:S(2)}) async-start(s8[6553600]{0:T(1024)(128)(4,1)} %bitcast.13), calls=%async_computation.2 | async-start | bytes 4718592
Sparse Core Ops, SparseCore 0:
  63.0 164.9 all-reduce.2
where the time goes:
time: 246 us
  waiting for transfers between devices  175 us (71%)
  Pallas kernels  40.8 us (17%)
  between operations  14.1 us (6%)
  other arithmetic  10.5 us (4%)
  starting transfers between devices  4.59 us (2%)
    psum x1, waiting for transfers between devices, shards(): grel, ghub = lax.psum((grel, ghub), ('blk', 'sub'))  165 us
    pallas_call x1, Pallas kernels, shards(): pl.pallas_call(functools.partial(first, w), out_shape=outs, in_specs=[vm]...  30.1 us
    pallas_call x1, Pallas kernels, shards(): pl.pallas_call(functools.partial(second, w), out_shape=outs, in_specs=[vm...  10.6 us
    ppermute x2, waiting for transfers between devices, shards(): lax.ppermute((right1, rs1), 'blk', [(i, (i + 1) % n) for i in range(n)])  9.35 us
    sub x2, other arithmetic, step(): return table - RATE * grads / jnp.sqrt(new)[None, :]  7.9 us
  transfers between devices with their start and end apart: 3, of which 2 were waited for; matrix products, arithmetic and copies ran while one was open for 0% of the time, Pallas kernels for 0%

commit v1 on v0

v1 whole, which is shorter than its diff:
```python
import functools
import jax
import jax.numpy as jnp
from jax import lax
from jax.experimental import pallas as pl
from jax.experimental.pallas import tpu as pltpu
from jax.sharding import PartitionSpec as P

RATE = 0.25
F32, BF16 = jnp.float32, jnp.bfloat16
NN = (((1,), (0,)), ((), ()))
NT = (((1,), (1,)), ((), ()))


def mm(a, b, dims=NN):
    return lax.dot_general(a, b, dims, preferred_element_type=F32)


def halves(x):
    hi = x.astype(BF16)
    return hi, (x - hi.astype(F32)).astype(BF16)


def stacked(x):
    hi, lo = halves(x)
    return jnp.concatenate([hi, lo], axis=0)


def mm3(a2, b_hi, b_lo, dims=NN):
    n = a2.shape[0] // 2
    both = mm(a2, b_hi, dims)
    return both[:n] + both[n:] + mm(a2[:n], b_lo, dims)


def fold(x):
    n = x.shape[0] // 2
    return x[:n] + x[n:]


def rows_hot(idx, base, count):
    at = lax.broadcasted_iota(jnp.int32, (count, idx.shape[1]), 0) + base
    return (at == idx).astype(F32).astype(BF16)


def column(idx):
    parts = []
    for k in range(0, idx.shape[1], 128):
        parts.append(jnp.broadcast_to(idx[:, k : k + 128], (128, 128)).T)
    return jnp.concatenate(parts, axis=0)


def lanes_hot(col, base, count):
    at = lax.broadcasted_iota(jnp.int32, (col.shape[0], 128), 1)
    return jnp.concatenate([col == at + (base + k) for k in range(0, count, 128)], axis=1)


def adagrad(table, state, grad):
    new_state = state + jnp.sum(grad * grad, axis=0, keepdims=True) * (1.0 / grad.shape[0])
    return table - grad * (RATE / jnp.sqrt(new_state)), new_state


def sigmoid(x):
    return 1.0 / (1.0 + jnp.exp(-x))


def cmul(a, b):
    n = a.shape[0] // 2
    a0, a1, b0, b1 = a[:n], a[n:], b[:n], b[n:]
    return jnp.concatenate([a0 * b0 - a1 * b1, a0 * b1 + a1 * b0], axis=0)


def cmul_conj(a, b):
    n = a.shape[0] // 2
    a0, a1, b0, b1 = a[:n], a[n:], b[:n], b[n:]
    return jnp.concatenate([a0 * b0 + a1 * b1, a1 * b0 - a0 * b1], axis=0)


def gather_loop(table_ref, idx, out_ref, block):
    count = table_ref.shape[1]
    out_ref[...] = jnp.zeros_like(out_ref)

    @pl.loop(0, count // block)
    def _(k):
        base = pl.multiple_of(k * block, block)
        out_ref[...] += mm(stacked(table_ref[:, pl.ds(base, block)]), rows_hot(idx, base, block))


def gather(table, idx):
    return mm(stacked(table), rows_hot(idx, 0, table.shape[1]))


def queries_side(q):
    qt = q.T
    return stacked(qt)


def first_right(w, left_ref, right_ref, rstate_ref, rel_ref, heads_ref, rels_ref, tails_ref, negs_ref,
                right_out, rstate_out, h0_out, r_out, q0_out, c_out, r_ref):
    rows = left_ref.shape[1]
    e = heads_ref.shape[1]
    right = right_ref[...]
    idx_r = jnp.concatenate([rels_ref[0:1, :], rels_ref[1:2, :]], axis=1)
    gather_loop(rel_ref, idx_r, r_ref, 256)
    r_out[...] = fold(r_ref[...])
    h0 = fold(gather(left_ref[...], heads_ref[0:1, :]))
    r0 = r_out[:, :e]
    q0 = cmul(h0, r0)
    h0_out[...] = h0
    q0_out[...] = q0
    rh, rl = halves(right)
    coef = coefs(mm3(stacked(q0.T), rh, rl), w, tails_ref[0:1, :], negs_ref[0:1, :], rows)
    c_out[...] = coef
    ch, cl = halves(coef)
    right_out[...], rstate_out[...] = adagrad(right, rstate_ref[...], mm3(stacked(q0), ch, cl))


def first_left(w, left_ref, lstate_ref, right_ref, hub_ref, heads_ref, hubs_ref, h0_ref, r_ref, q0_ref, c_ref,
               left_out, lstate_out, h1_out, q1_out, dqh1_out, dr0_out, du_ref, u_ref):
    rows = left_ref.shape[1]
    feats = left_ref.shape[0]
    e = heads_ref.shape[1]
    left = left_ref[...]
    q0 = q0_ref[...]
    r0 = r_ref[:, :e]
    q0t = stacked(q0.T)
    q02 = stacked(q0)
    idx_u = jnp.concatenate([hubs_ref[0:1, :], hubs_ref[1:2, :]], axis=1)
    gather_loop(hub_ref, idx_u, u_ref, 512)
    m = hubs_ref.shape[1]
    u0h, u0l = u_ref[:feats, :m].astype(BF16), u_ref[feats:, :m].astype(BF16)
    ch2, cl2 = halves(sigmoid(mm3(q0t, u0h, u0l)) * w)
    du_ref[:feats, :m] = mm3(q02, ch2, cl2)
    ch, cl = halves(c_ref[...])
    u2 = jnp.concatenate([u0h, u0l], axis=0)
    dq = mm3(stacked(right_ref[...]), ch, cl, NT) + mm3(u2, ch2, cl2, NT)
    dh = cmul_conj(dq, r0)
    dr0_out[...] = cmul_conj(dq, h0_ref[...])
    gl = fold(mm(stacked(dh), lanes_hot(column(heads_ref[0:1, :]), 0, rows).astype(F32).astype(BF16)))
    left1, lstate_out[...] = adagrad(left, lstate_ref[...], gl)
    left_out[...] = left1
    h1 = fold(gather(left1, heads_ref[1:2, :]))
    q1 = cmul(h1, r_ref[:, e:])
    h1_out[...] = h1
    q1_out[...] = q1
    u1h, u1l = u_ref[:feats, m:].astype(BF16), u_ref[feats:, m:].astype(BF16)
    ch3, cl3 = halves(sigmoid(mm3(stacked(q1.T), u1h, u1l)) * w)
    du_ref[:feats, m:] = mm3(stacked(q1), ch3, cl3)
    dqh1_out[...] = mm3(jnp.concatenate([u1h, u1l], axis=0), ch3, cl3, NT)
    du_ref[feats:, :] = jnp.broadcast_to(idx_u.astype(F32), (8, 2 * m))


def coefs(score, w, tail_idx, neg_idx, rows):
    times = jnp.sum(rows_hot_f(neg_idx, rows), axis=1, keepdims=True)
    times = jnp.broadcast_to(times, (rows, 128)).T[0:1, :] * w
    tail = lanes_hot(column(tail_idx), 0, rows)
    s = sigmoid(score)
    return s * times + jnp.where(tail, s - 1.0, 0.0)


def rows_hot_f(idx, count):
    at = lax.broadcasted_iota(jnp.int32, (count, idx.shape[1]), 0)
    return (at == idx).astype(F32)


HT, RT = 17, 6
MESH = pl.DeviceIdType.MESH


class Place:
    def __init__(self):
        b, s = lax.axis_index("blk"), lax.axis_index("sub")
        self.core = lax.rem(b, 2)
        self.pos = [b // 4, lax.rem(b // 2, 2) * 2 + lax.rem(s, 2), s // 2]

    def at(self, pos, core):
        return ((pos[0] * 2 + pos[1] // 2) * 2 + core, pos[2] * 2 + lax.rem(pos[1], 2))

    def shift(self, axis, d):
        pos = list(self.pos)
        pos[axis] = lax.rem(pos[axis] + d, 4)
        return self.at(pos, self.core)

    def sibling(self):
        return self.at(self.pos, 1 - self.core)


class Reduce:
    def __init__(self, place, n, g, rb1, s1, rb2, s2, rb3, full, sems):
        self.p, self.n = place, n
        self.g, self.rb1, self.s1, self.rb2, self.s2, self.rb3, self.full = g, rb1, s1, rb2, s2, rb3, full
        self.sems = sems
        self.live = {}

    def copy(self, stage, part, k, src, dst, dev):
        return pltpu.make_async_remote_copy(
            src_ref=src, dst_ref=dst, send_sem=self.sems.at[0, stage, part, k], recv_sem=self.sems.at[1, stage, part, k],
            device_id=dev, device_id_type=MESH)

    def put(self, stage, part, k, src, dst, dev):
        c = self.copy(stage, part, k, src, dst, dev)
        c.start()
        self.live[stage, part, k] = c

    def axis(self, part, level):
        return (part + level) % 3

    def here(self, part, level):
        return self.p.pos[self.axis(part, level)]

    def rs1(self, part):
        n, c, a = self.n, self.here(part, 0), self.axis(part, 0)
        for d in (2, 1, 3):
            off = part * 16 * n + lax.rem(c + d, 4) * (4 * n)
            self.put(0, part, d - 1, self.g.at[pl.ds(off, 4 * n)], self.rb1.at[part, d - 1], self.p.shift(a, d))

    def rs1_done(self, part):
        n, c = self.n, self.here(part, 0)
        for d in (1, 3, 2):
            self.live[0, part, d - 1].wait_recv()
        off = part * 16 * n + c * (4 * n)
        self.s1[part] = (self.g[pl.ds(off, 4 * n)] + self.rb1[part, 0]) + (self.rb1[part, 1] + self.rb1[part, 2])

    def rs2(self, part):
        n, c, a = self.n, self.here(part, 1), self.axis(part, 1)
        for d in (2, 1, 3):
            self.put(1, part, d - 1, self.s1.at[part, pl.ds(lax.rem(c + d, 4) * n, n)], self.rb2.at[part, d - 1],
                     self.p.shift(a, d))

    def rs2_done(self, part):
        n, c = self.n, self.here(part, 1)
        for d in (1, 3, 2):
            self.live[1, part, d - 1].wait_recv()
        self.s2[part] = (self.s1[part, pl.ds(c * n, n)] + self.rb2[part, 0]) + (self.rb2[part, 1] + self.rb2[part, 2])

    def ar3(self, part):
        c, a = self.here(part, 2), self.axis(part, 2)
        for d in (2, 1, 3):
            self.put(2, part, d - 1, self.s2.at[part], self.rb3.at[part, c], self.p.shift(a, d))
        self.rb3[part, c] = self.s2[part]

    def mine(self, part):
        n = self.n
        return part * 16 * n + self.here(part, 0) * (4 * n) + self.here(part, 1) * n

    def ar3_done(self, part):
        for d in (1, 3, 2):
            self.live[2, part, d - 1].wait_recv()
        self.full[self.p.core, pl.ds(self.mine(part), self.n)] = (
            (self.rb3[part, 0] + self.rb3[part, 1]) + (self.rb3[part, 2] + self.rb3[part, 3]))

    def ag2(self, part):
        a = self.axis(part, 1)
        ref = self.full.at[self.p.core, pl.ds(self.mine(part), self.n)]
        for d in (2, 1, 3):
            self.put(3, part, d - 1, ref, ref, self.p.shift(a, d))

    def ag2_done(self, part):
        for d in (1, 3, 2):
            self.live[3, part, d - 1].wait_recv()

    def chunk(self, part, c):
        return self.full.at[self.p.core, pl.ds(part * 16 * self.n + c * (4 * self.n), 4 * self.n)]

    def ag1(self, part):
        c, a = self.here(part, 0), self.axis(part, 0)
        ref = self.chunk(part, c)
        for d in (2, 1, 3):
            self.put(4, part, d - 1, ref, ref, self.p.shift(a, d))
        self.put(5, part, 3, ref, ref, self.p.sibling())

    def ag1_done(self, part):
        c = self.here(part, 0)
        for d in (1, 3, 2):
            self.live[4, part, d - 1].wait_recv()
            ref = self.chunk(part, lax.rem(c + 4 - d, 4))
            self.put(5, part, d - 1, ref, ref, self.p.sibling())

    def finish(self, part):
        for k in range(4):
            self.live[5, part, k].wait_recv()
        for c in self.live:
            if c[1] == part:
                self.live[c].wait_send()


def tiles_of(x):
    return [x[:, k : k + 128].reshape(x.shape[0] // 8, 8, 128) for k in range(0, x.shape[1], 128)]


def scatter_into(g_ref, at, grad2, col, base, width, add):
    hot = lanes_hot(col, base, width).astype(F32).astype(BF16)
    for j, t in enumerate(tiles_of(fold(mm(grad2, hot)))):
        n = t.shape[0]
        here = pl.ds(at + j * n, n)
        g_ref[here] = g_ref[here] + t if add else t


def second(w, du_ref, dr0_ref, left_ref, lstate_ref, right_ref, rstate_ref, h1_ref, r_ref, q1_ref, dqh1_ref,
           heads_ref, rels_ref, tails_ref, negs_ref, left_out, right_out, ghub_out, grel_out,
           dus, dro, drs, hg, hrb1, hs1, hrb2, hs2, hrb3, hfull, rg, rrb1, rs1, rrb2, rs2, rrb3, rfull, hsem, rsem,
           xsem, osem):
    place = Place()
    feats, rows = left_ref.shape
    e = q1_ref.shape[1]
    hub = Reduce(place, HT, hg, hrb1, hs1, hrb2, hs2, hrb3, hfull, hsem)
    rel = Reduce(place, RT, rg, rrb1, rs1, rrb2, rs2, rrb3, rfull, rsem)
    barrier = pltpu.get_barrier_semaphore()
    for a in range(3):
        for d in (1, 2, 3):
            pl.semaphore_signal(barrier, inc=1, device_id=place.shift(a, d), device_id_type=MESH)
    pl.semaphore_signal(barrier, inc=1, device_id=place.sibling(), device_id_type=MESH)
    pl.semaphore_wait(barrier, 10)

    def to_sibling(k, src, dst):
        c = pltpu.make_async_remote_copy(src_ref=src, dst_ref=dst, send_sem=xsem.at[0, k], recv_sem=xsem.at[1, k],
                                         device_id=place.sibling(), device_id_type=MESH)
        c.start()
        return c

    x_u = to_sibling(0, du_ref, dus)
    dro[0, :feats, :] = dr0_ref[...]
    dro[0, feats:, :] = jnp.broadcast_to(rels_ref[0:1, :].astype(F32), (8, e))
    x_r0 = to_sibling(1, dro.at[0], drs.at[0])

    hub_lanes = 2048
    first_lane = place.core * hub_lanes
    own2 = stacked(du_ref[:feats, :])
    own_col = column(du_ref[feats : feats + 1, :].astype(jnp.int32))
    for k in range(4):
        scatter_into(hg, k * 200, own2, own_col, first_lane + k * 512, 512, False)
    hg[800:, :, :] = jnp.zeros((48 * HT - 800, 8, 128), F32)
    x_u.wait_recv()
    sib2 = stacked(dus[:feats, :])
    sib_col = column(dus[feats : feats + 1, :].astype(jnp.int32))
    for k in range(4):
        scatter_into(hg, k * 200, sib2, sib_col, first_lane + k * 512, 512, True)
        if k:
            hub.rs1(k - 1)

    right = right_ref[...]
    q1 = q1_ref[...]
    rh, rl = halves(right)
    coef = coefs(mm3(stacked(q1.T), rh, rl), w, tails_ref[1:2, :], negs_ref[1:2, :], rows)
    ch, cl = halves(coef)
    dq = mm3(jnp.concatenate([rh, rl], axis=0), ch, cl, NT) + dqh1_ref[...]
    dro[1, :feats, :] = cmul_conj(dq, h1_ref[...])
    dro[1, feats:, :] = jnp.broadcast_to(rels_ref[1:2, :].astype(F32), (8, e))
    x_r1 = to_sibling(2, dro.at[1], drs.at[1])
    rel_lanes = 640
    first_rel = place.core * rel_lanes
    x_r0.wait_recv()

    def rel_scatter(x, add):
        scatter_into(rg, 0, stacked(x[:feats, :]), column(x[feats : feats + 1, :].astype(jnp.int32)), first_rel, 640,
                     add)

    rel_scatter(dro[0], False)
    rel_scatter(drs[0], True)
    rel_scatter(dro[1], True)
    rg[250:, :, :] = jnp.zeros((48 * RT - 250, 8, 128), F32)
    x_r1.wait_recv()
    rel_scatter(drs[1], True)
    for p in range(3):
        rel.rs1(p)
    for p in range(3):
        hub.rs1_done(p)
        hub.rs2(p)
    g = mm3(stacked(q1), ch, cl)
    right_out[...], _ = adagrad(right, rstate_ref[...], g)
    for p in range(3):
        rel.rs1_done(p)
        rel.rs2(p)
    for p in range(3):
        hub.rs2_done(p)
        hub.ar3(p)
    dh = cmul_conj(dq, r_ref[:, e:])
    gl = fold(mm(stacked(dh), lanes_hot(column(heads_ref[1:2, :]), 0, rows).astype(F32).astype(BF16)))
    left_out[...], _ = adagrad(left_ref[...], lstate_ref[...], gl)
    for p in range(3):
        hub.ar3_done(p)
        hub.ag2(p)
    for p in range(3):
        rel.rs2_done(p)
        rel.ar3(p)
    for p in range(3):
        hub.ag2_done(p)
        hub.ag1(p)
    for p in range(3):
        rel.ar3_done(p)
        rel.ag2(p)
    for p in range(3):
        rel.ag2_done(p)
        rel.ag1(p)
    for p in range(3):
        hub.ag1_done(p)
    for p in range(3):
        rel.ag1_done(p)
    for p in range(3):
        hub.finish(p)
        rel.finish(p)
    x_u.wait_send()
    x_r0.wait_send()
    x_r1.wait_send()
    a = pltpu.make_async_copy(hfull, ghub_out, osem.at[0])
    b = pltpu.make_async_copy(rfull, grel_out, osem.at[1])
    a.start()
    b.start()
    a.wait()
    b.wait()


def update(table_ref, state_ref, g_ref, out_ref):
    for j in range(table_ref.shape[1] // 128):
        lanes = slice(j * 128, (j + 1) * 128)
        n = table_ref.shape[0] // 8
        g = g_ref[0, j * n : (j + 1) * n].reshape(table_ref.shape[0], 128)
        new = state_ref[:, lanes] + jnp.sum(g * g, axis=0, keepdims=True) * (1.0 / table_ref.shape[0])
        out_ref[:, lanes] = table_ref[:, lanes] - g * (RATE / jnp.sqrt(new))


def apply(table, state, g, width, name):
    feats, lanes = table.shape
    per = lanes // 2 // width
    at = lambda h, k: (0, h * per + k)
    return pl.pallas_call(
        update, out_shape=jax.ShapeDtypeStruct(table.shape, F32), grid=(2, per),
        in_specs=[pl.BlockSpec((feats, width), at), pl.BlockSpec((1, width), at),
                  pl.BlockSpec((1, feats // 8 * width // 128, 8, 128), lambda h, k: (h, k, 0, 0))],
        out_specs=pl.BlockSpec((feats, width), at), name=name,
        compiler_params=pltpu.CompilerParams(vmem_limit_bytes=40 * 2**20),
    )(table, state[None], g)


def shards(left_emb, left_state, right_emb, right_state, relation_emb, relation_state, hub_emb, hub_state, heads,
           relations, tails, negatives, hub_ids):
    two, half, rows = left_emb.shape
    feats = two * half
    e = heads.shape[1]
    m = hub_ids.shape[1]
    w = 1.0 / (negatives.shape[1] + hub_ids.shape[1])
    left = left_emb.reshape(feats, rows)
    right = right_emb.reshape(feats, rows)
    rel = relation_emb.reshape(feats, -1)
    hub = hub_emb.reshape(feats, -1)
    sd = lambda *s: jax.ShapeDtypeStruct(s, F32)
    vm = pl.BlockSpec(memory_space=pltpu.VMEM)
    hbm = pl.BlockSpec(memory_space=pl.ANY)
    params = pltpu.CompilerParams(vmem_limit_bytes=50 * 2**20)
    outs = [sd(feats, rows), sd(1, rows), sd(feats, e), sd(feats, 2 * e), sd(feats, e), sd(e, rows)]
    right1, rs1, h0, r, q0, c0 = pl.pallas_call(
        functools.partial(first_right, w), out_shape=outs, in_specs=[vm] * 8, out_specs=[vm] * len(outs),
        scratch_shapes=[pltpu.VMEM((2 * feats, 2 * e), F32)],
        compiler_params=params, name="first_right",
        cost_estimate=pl.CostEstimate(flops=6 * 10**9, bytes_accessed=10**7, transcendentals=0),
    )(left, right, right_state[None], rel, heads, relations, tails, negatives)
    n = lax.axis_size("blk")
    right1, rs1 = lax.ppermute((right1, rs1), "blk", [(i, (i + 1) % n) for i in range(n)])
    outs = [sd(feats, rows), sd(1, rows), sd(feats, e), sd(feats, e), sd(feats, e), sd(feats, e), sd(feats + 8, 2 * m)]
    left1, ls1, h1, q1, dqh1, dr0, du = pl.pallas_call(
        functools.partial(first_left, w), out_shape=outs, in_specs=[vm] * 10, out_specs=[vm] * len(outs),
        scratch_shapes=[pltpu.VMEM((2 * feats, 2 * m), F32)],
        compiler_params=params, name="first_left",
        cost_estimate=pl.CostEstimate(flops=10 * 10**9, bytes_accessed=4 * 10**7, transcendentals=0),
    )(left, left_state[None], right, hub, heads, hub_ids, h0, r, q0, c0)
    tile = lambda *s: pltpu.VMEM((*s, 8, 128), F32)
    stage = lambda n: [tile(48 * n), tile(3, 3, 4 * n), tile(3, 4 * n), tile(3, 3, n), tile(3, n), tile(3, 4, n),
                       tile(2, 48 * n)]
    outs = [sd(feats, rows), sd(feats, rows), sd(2, 48 * HT, 8, 128), sd(2, 48 * RT, 8, 128)]
    left2, right2, ghub, grel = pl.pallas_call(
        functools.partial(second, w), out_shape=outs, in_specs=[vm] * 14, out_specs=[vm, vm, hbm, hbm],
        scratch_shapes=[pltpu.VMEM((feats + 8, 2 * m), F32), pltpu.VMEM((2, feats + 8, e), F32),
                        pltpu.VMEM((2, feats + 8, e), F32), *stage(HT), *stage(RT),
                        pltpu.SemaphoreType.DMA((2, 6, 3, 4)), pltpu.SemaphoreType.DMA((2, 6, 3, 4)),
                        pltpu.SemaphoreType.DMA((2, 3)), pltpu.SemaphoreType.DMA((2,))],
        compiler_params=pltpu.CompilerParams(vmem_limit_bytes=56 * 2**20, collective_id=1, has_side_effects=True),
        name="second_bucket_and_sums",
    )(du, dr0, left1, ls1, right1, rs1, h1, r, q1, dqh1, heads, relations, tails, negatives)
    rel_new = apply(rel, relation_state, grel, 640, "relation_update")
    hub_new = apply(hub, hub_state, ghub, 512, "hub_update")
    return (left2.reshape(left_emb.shape), right2.reshape(right_emb.shape), rel_new.reshape(relation_emb.shape),
            hub_new.reshape(hub_emb.shape))


def solution(mesh):
    cut = P(None, None, ("blk", "sub"))
    row = P(("blk", "sub"))
    idx = P(None, ("blk", "sub"))
    return jax.shard_map(shards, mesh=mesh, in_specs=(cut, row, cut, row, P(), P(), P(), P(), idx, idx, idx, idx, idx),
                         out_specs=(cut, cut, P(), P()), check_vma=False)
```

time: 246 us -> 131 us (0.53)
  waiting for transfers between devices: 175 us -> 0.01 us
  Pallas kernels: 40.8 us -> 108 us
  local copies, waits for them, and re-layouts: 1.34 us -> 17.6 us
  between operations: 14.1 us -> 0.76 us
  other arithmetic: 10.5 us -> 0.01 us
    psum x1 -> x0, waiting for transfers between devices: 165 us -> none  [shards(): grel, ghub = lax.psum((grel, ghub), ('blk', 'sub'))]
    pallas_call x1, Pallas kernels: 10.6 us -> 75.4 us  [shards(): pl.pallas_call(functools.partial(second, w), out_shape=outs, in_specs=[vm...]
    unnamed x16 -> x60, local copies, waits for them, and re-layouts: 1.34 us -> 17.6 us
    ppermute x2, waiting for transfers between devices: 9.35 us -> 0.01 us  [shards(): lax.ppermute((right1, rs1), 'blk', [(i, (i + 1) % n) for i in range(n)])]
    sub x2 -> x0, other arithmetic: 7.9 us -> none  [step(): return table - RATE * grads / jnp.sqrt(new)[None, :]]
    pallas_call x1 -> x4, Pallas kernels: 30.1 us -> 33 us  [the longest x1 16.9 us: shards(): pl.pallas_call(functools.partial(first_left, w), out_shape=outs, in_specs...]
    reduce_sum x2 -> x0, other arithmetic: 2.57 us -> none  [step(): new = state + jnp.mean(grads * grads, axis=0)]
  transfers between devices with their start and end apart: 3 -> 2, of which waited for: 2 -> 0; matrix products, arithmetic and copies ran while one was open for 0% -> 0% of each run, Pallas kernels for 0% -> 13%
where the time goes in v1:
time: 131 us
  Pallas kernels  108 us (82%)
  local copies, waits for them, and re-layouts  17.6 us (13%)
  starting transfers between devices  4.34 us (3%)
    pallas_call x1, Pallas kernels, shards(): pl.pallas_call(functools.partial(second, w), out_shape=outs, in_specs=[vm...  75.4 us
    unnamed x60, local copies, waits for them, and re-layouts  17.6 us
    pallas_call x1, Pallas kernels, shards(): pl.pallas_call(functools.partial(first_left, w), out_shape=outs, in_specs...  16.9 us
    pallas_call x1, Pallas kernels, shards(): pl.pallas_call(functools.partial(first_right, w), out_shape=outs, in_spec...  9.23 us
    pallas_call x2, Pallas kernels, apply(): pl.pallas_call(update, out_shape=jax.ShapeDtypeStruct(table.shape, F32),...  6.83 us
    ppermute x2, starting transfers between devices, shards(): lax.ppermute((right1, rs1), 'blk', [(i, (i + 1) % n) for i in range(n)])  4.34 us
  transfers between devices with their start and end apart: 2, of which 0 were waited for; matrix products, arithmetic and copies ran while one was open for 0% of the time, Pallas kernels for 13%

profile of v1, /device:TPU:1, one launch (start us, length us, event | category | flops | bytes accessed | tf_op | source)
XLA Modules:
  0.0 131.0 jit_solution(6756839951885564300)
XLA Ops:
  0.6 0.0 copy-start.9
  0.6 0.7 copy-done.9
  1.3 0.7 copy-done.10
  2.0 0.0 copy-start.12
  2.0 0.7 copy-done.12
  2.7 0.0 copy-start.13
  2.7 0.7 copy-done.13
  3.4 0.0 copy-start.15
  3.4 1.1 copy-done.15
  4.5 1.1 copy-done.16
  5.7 0.7 copy-done.17
  6.4 9.2 %first_right.1 = (f32[400,512]{1,0:T(8,128)S(1)}, f32[1,512]{1,0:T(1,128)S(1)}, f32[400,512]{1,0:T(8,128)S(1)}, f32[400,1024]{1,0:T(8,128)}, f32[400,512]{1,0:T(8,128)S(1)}, /*index=5*/f32[512,512]{1,0:T(8,128)}) custom-call(f32[400,512]{1,0:T(8,128)S(1)} %bitcast.19, f32[400,512]{1,0:T(8,128)S(1)} %bitcast.21, f32[1,512]{1,0:T(1,128)S(1)} %bitcast.22, ...), custom_call_target="tpu_custom_call" | custom-call | flops 6000000000 | bytes 10000000 | tf_op jit(solution)/shard_map/first_right/pallas_call | solution.py:450
  15.6 0.9 copy-done.20
  16.5 0.9 copy-done.21
  17.4 4.3 %collective-permute-start = (f32[400,512]{1,0:T(8,128)S(1)}, f32[400,512]{1,0:T(8,128)S(1)}, u32[]{:S(2)}, u32[]{:S(2)}) collective-permute-start(f32[400,512]{1,0:T(8,128)S(1)} %get-tuple-element.29), channel_id=1, source_target_pairs={{0,8},{8,16},{16,24},{24,32},{32,40},{40,48},{48,56},{56,64},{64,7... | collective-permute-start | bytes 2457608 | tf_op jit(solution)/shard_map/ppermute | solution.py:457
  21.7 0.0 collective-permute-start.1
  21.7 0.0 copy-done.11
  21.7 0.0 copy-done.18
  21.7 0.0 copy-done.19
  21.7 0.0 slice-start.1
  21.8 16.9 %first_left.1 = (f32[400,512]{1,0:T(8,128)S(1)}, f32[1,512]{1,0:T(1,128)S(1)}, f32[400,512]{1,0:T(8,128)S(1)}, f32[400,512]{1,0:T(8,128)S(1)}, f32[400,512]{1,0:...) custom-call(f32[400,512]{1,0:T(8,128)} %bitcast.18, f32[1,512]{1,0:T(1,128)S(1)} %bitcast.23, ...), custom_call_target="tpu_custom_call" | custom-call | flops 10000000000 | bytes 40000000 | tf_op jit(solution)/shard_map/first_left/pallas_call | solution.py:459
  38.7 0.9 copy-done.3
  39.5 0.9 copy-done.4
  40.4 0.9 copy-done.5
  41.3 0.9 copy-done.6
  42.2 0.9 copy-done.7
  43.1 0.0 copy-done.25
  43.1 0.0 collective-permute-done.1.rstate_ref
  43.1 0.0 copy-start.26
  43.2 0.0 collective-permute-done.right_ref
  43.2 0.0 copy-start.24
  43.2 0.5 copy-done.14
  43.7 0.0 copy-done.26
  43.7 0.3 copy-done.24
  44.1 75.4 %second_bucket_and_sums.1 = (f32[400,512]{1,0:T(8,128)}, f32[400,512]{1,0:T(8,128)}, f32[2,816,8,128]{3,2,1,0:T(8,128)}, f32[2,288,8,128]{3,2,1,0:T(8,128)}) custom-call(f32[408,512]{1,0:T(8,128)} %get-tuple-element.25.du_ref, f32[400,512]{1,0:T(8,128)} %copy-done.7, f32[400,512]{1,0:T(8,128)} %copy-done.3, f32[1,512]{1,0:T(1,128)} %copy-done.14, ...), custom_call_target="tpu_custom_call" | custom-call | tf_op jit(solution)/shard_map/second_bucket_and_sums/pallas_call | solution.py:469
  119.5 0.0 slice-done
  119.5 0.0 slice-done.1
  119.5 0.0 copy-done.8
  119.5 0.0 copy-start
  119.5 2.9 %copy-done = f32[2,816,8,128]{3,2,1,0:T(8,128)S(1)} copy-done((f32[2,816,8,128]{3,2,1,0:T(8,128)S(1)}, f32[2,816,8,128]{3,2,1,0:T(8,128)}, u32[]{:S(2)}) %copy-start) | copy-done | bytes 6684696
  122.4 5.1 %hub_update.1 = f32[400,4096]{1,0:T(8,128)} custom-call(f32[400,4096]{1,0:T(8,128)S(1)} %bitcast.14, f32[1,4096]{1,0:T(1,128)S(1)} %bitcast.17, f32[2,816,8,128]{3,2,1,0:T(8,128)S(1)} %copy-done), custom_call_target="tpu_custom_call" | custom-call | tf_op jit(solution)/shard_map/hub_update/pallas_call | solution.py:425
  127.5 0.0 copy-done.1
  127.5 0.0 copy-done.2
  127.5 1.7 %relation_update.1 = f32[400,1280]{1,0:T(8,128)} custom-call(f32[400,1280]{1,0:T(8,128)S(1)} %bitcast.16, f32[1,1280]{1,0:T(1,128)S(1)} %broadcast_in_dim.14.state_ref, f32[2,288,8,128]{3,2,1,0:T(8,128)S(1)} %copy-done.1), custom_call_target="tpu_custom_call" | custom-call | tf_op jit(solution)/shard_map/relation_update/pallas_call | solution.py:425
  129.2 0.0 copy-done.23
  129.2 0.9 copy.19
  130.1 0.0 copy-done.22
  130.1 0.9 copy.20
  (23 shorter events, 0.0 us)
Async XLA Ops:
  0.6 0.7 copy-start.9
  1.3 0.7 copy-start.10
  2.0 0.7 copy-start.12
  2.7 0.7 copy-start.13
  3.4 1.1 copy-start.15
  4.5 1.1 copy-start.16
  5.7 0.7 copy-start.17
  6.4 15.4 %copy-start.11 = (s32[2,512]{1,0:T(2,128)S(1)}, s32[2,512]{1,0:T(2,128)}, u32[]{:S(2)}) copy-start(s32[2,512]{1,0:T(2,128)} %heads_ref.5) | copy-start | bytes 12292
  6.4 15.4 %copy-start.18 = (f32[512]{0:T(512)S(1)}, f32[512]{0:T(512)}, u32[]{:S(2)}) copy-start(f32[512]{0:T(512)} %param.14) | copy-start | bytes 6148
  6.4 15.4 %copy-start.19 = (s32[2,256]{1,0:T(2,128)S(1)}, s32[2,256]{1,0:T(2,128)}, u32[]{:S(2)}) copy-start(s32[2,256]{1,0:T(2,128)} %hubs_ref.1) | copy-start | bytes 6148
  6.4 113.1 %slice-start = ((s8[6553600]{0:T(1024)(128)(4,1)}), s8[4194304]{0:T(1024)(128)(4,1)S(1)}, s32[]{:S(2)}) async-start(s8[6553600]{0:T(1024)(128)(4,1)} %bitcast.12), calls=%async_computation | async-start | bytes 8388608
  15.6 0.9 copy-start.20
  16.5 0.9 copy-start.21
  17.4 25.8 %collective-permute-start = (f32[400,512]{1,0:T(8,128)S(1)}, f32[400,512]{1,0:T(8,128)S(1)}, u32[]{:S(2)}, u32[]{:S(2)}) collective-permute-start(f32[400,512]{1,0:T(8,128)S(1)} %get-tuple-element.29), channel_id=1, source_target_pairs={{0,8},{8,16},{16,24},{24,32},{32,40},{40,48},{48,56},{56,64},{64,7... | collective-permute-start | bytes 2457608 | tf_op jit(solution)/shard_map/ppermute | solution.py:457
  21.7 21.4 %collective-permute-start.1 = (f32[1,512]{1,0:T(1,128)S(1)}, f32[1,512]{1,0:T(1,128)S(1)}, u32[]{:S(2)}, u32[]{:S(2)}) collective-permute-start(f32[1,512]{1,0:T(1,128)S(1)} %get-tuple-element.30), channel_id=1, source_target_pairs={{0,8},{8,16},{16,24},{24,32},{32,40},{40,48},{48,56},{56,64},{64,7... | collective-permute-start | bytes 6152 | tf_op jit(solution)/shard_map/ppermute | solution.py:457
  21.7 21.4 %copy-start.25 = (f32[1280]{0:T(1024)S(1)}, f32[1280]{0:T(1024)}, u32[]{:S(2)}) copy-start(f32[1280]{0:T(1024)} %param.18) | copy-start | bytes 15364
  21.7 97.7 %slice-start.1 = ((s8[6553600]{0:T(1024)(128)(4,1)}), s8[2359296]{0:T(1024)(128)(4,1)S(1)}, s32[]{:S(2)}) async-start(s8[6553600]{0:T(1024)(128)(4,1)} %bitcast.12), calls=%async_computation.1 | async-start | bytes 4718592
  38.7 0.9 copy-start.3
  39.5 0.9 copy-start.4
  40.4 0.9 copy-start.5
  41.3 0.9 copy-start.6
  42.2 0.9 copy-start.7
  43.1 0.6 copy-start.14
  43.1 0.6 copy-start.26
  43.2 0.9 copy-start.24
  44.1 75.4 %copy-start.8 = (f32[4096]{0:T(1024)S(1)}, f32[4096]{0:T(1024)}, u32[]{:S(2)}) copy-start(f32[4096]{0:T(1024)} %param.20) | copy-start | bytes 49156
  119.5 2.9 %copy-start = (f32[2,816,8,128]{3,2,1,0:T(8,128)S(1)}, f32[2,816,8,128]{3,2,1,0:T(8,128)}, u32[]{:S(2)}) copy-start(f32[2,816,8,128]{3,2,1,0:T(8,128)} %get-tuple-element.37.g_ref) | copy-start | bytes 20054020
  122.4 5.2 %copy-start.1 = (f32[2,288,8,128]{3,2,1,0:T(8,128)S(1)}, f32[2,288,8,128]{3,2,1,0:T(8,128)}, u32[]{:S(2)}) copy-start(f32[2,288,8,128]{3,2,1,0:T(8,128)} %get-tuple-element.36.g_ref) | copy-start | bytes 7077892
  122.4 5.2 %copy-start.2 = (f32[2,200,1280]{2,1,0:T(8,128)S(1)}, f32[2,200,1280]{2,1,0:T(8,128)}, u32[]{:S(2)}) copy-start(f32[2,200,1280]{2,1,0:T(8,128)} %param.17) | copy-start | bytes 6144004
  127.5 1.7 %copy-start.23 = (f32[400,512]{1,0:T(8,128)S(1)}, f32[400,512]{1,0:T(8,128)}, u32[]{:S(2)}) copy-start(f32[400,512]{1,0:T(8,128)} %get-tuple-element.34) | copy-start | bytes 2457604
  127.5 2.6 %copy-start.22 = (f32[400,512]{1,0:T(8,128)S(1)}, f32[400,512]{1,0:T(8,128)}, u32[]{:S(2)}) copy-start(f32[400,512]{1,0:T(8,128)} %get-tuple-element.35) | copy-start | bytes 2457604

commit v2 on v0

v2 whole, which is shorter than its diff:
```python
import functools
import jax
import jax.numpy as jnp
from jax import lax
from jax.experimental import pallas as pl
from jax.experimental.pallas import tpu as pltpu
from jax.sharding import PartitionSpec as P

RATE = 0.25
F32, BF16 = jnp.float32, jnp.bfloat16
NN = (((1,), (0,)), ((), ()))
NT = (((1,), (1,)), ((), ()))


def mm(a, b, dims=NN):
    return lax.dot_general(a, b, dims, preferred_element_type=F32)


def halves(x):
    hi = x.astype(BF16)
    return hi, (x - hi.astype(F32)).astype(BF16)


def stacked(x):
    hi, lo = halves(x)
    return jnp.concatenate([hi, lo], axis=0)


def mm3(a2, b_hi, b_lo, dims=NN):
    n = a2.shape[0] // 2
    both = mm(a2, b_hi, dims)
    return both[:n] + both[n:] + mm(a2[:n], b_lo, dims)


def fold(x):
    n = x.shape[0] // 2
    return x[:n] + x[n:]


def rows_hot(idx, base, count):
    at = lax.broadcasted_iota(jnp.int32, (count, idx.shape[1]), 0) + base
    return (at == idx).astype(F32).astype(BF16)


def column(idx):
    parts = []
    for k in range(0, idx.shape[1], 128):
        parts.append(jnp.broadcast_to(idx[:, k : k + 128], (128, 128)).T)
    return jnp.concatenate(parts, axis=0)


def lanes_hot(col, base, count):
    at = lax.broadcasted_iota(jnp.int32, (col.shape[0], 128), 1)
    return jnp.concatenate([col == at + (base + k) for k in range(0, count, 128)], axis=1)


def adagrad(table, state, grad):
    new_state = state + jnp.sum(grad * grad, axis=0, keepdims=True) * (1.0 / grad.shape[0])
    return table - grad * (RATE / jnp.sqrt(new_state)), new_state


def sigmoid(x):
    return 1.0 / (1.0 + jnp.exp(-x))


def cmul(a, b):
    n = a.shape[0] // 2
    a0, a1, b0, b1 = a[:n], a[n:], b[:n], b[n:]
    return jnp.concatenate([a0 * b0 - a1 * b1, a0 * b1 + a1 * b0], axis=0)


def cmul_conj(a, b):
    n = a.shape[0] // 2
    a0, a1, b0, b1 = a[:n], a[n:], b[:n], b[n:]
    return jnp.concatenate([a0 * b0 + a1 * b1, a1 * b0 - a0 * b1], axis=0)


def gather_loop(table_ref, idx, out_ref, block):
    count = table_ref.shape[1]
    out_ref[...] = jnp.zeros_like(out_ref)

    @pl.loop(0, count // block)
    def _(k):
        base = pl.multiple_of(k * block, block)
        out_ref[...] += mm(stacked(table_ref[:, pl.ds(base, block)]), rows_hot(idx, base, block))


def gather(table, idx):
    return mm(stacked(table), rows_hot(idx, 0, table.shape[1]))


def queries_side(q):
    qt = q.T
    return stacked(qt)


def coefs(score, w, tail_idx, neg_idx, rows):
    times = jnp.sum(rows_hot_f(neg_idx, rows), axis=1, keepdims=True)
    times = jnp.broadcast_to(times, (rows, 128)).T[0:1, :] * w
    tail = lanes_hot(column(tail_idx), 0, rows)
    s = sigmoid(score)
    return s * times + jnp.where(tail, s - 1.0, 0.0)


def rows_hot_f(idx, count):
    at = lax.broadcasted_iota(jnp.int32, (count, idx.shape[1]), 0)
    return (at == idx).astype(F32)


VMEM_MIB = 54
HUB_PARTS, REL_PARTS = (9, 8), (6,)
MESH = pl.DeviceIdType.MESH


class Sent:
    def __init__(self, src, dst, send_sem, recv_sem, dev, log):
        self.c = pltpu.make_async_remote_copy(src_ref=src, dst_ref=dst, send_sem=send_sem, recv_sem=recv_sem,
                                              device_id=dev, device_id_type=MESH)
        self.c.start()
        self.arrived = False
        log.append(self)

    def wait_recv(self):
        if not self.arrived:
            self.c.wait_recv()
            self.arrived = True

    def close(self):
        self.wait_recv()
        self.c.wait_send()


class Place:
    def __init__(self):
        b, s = lax.axis_index("blk"), lax.axis_index("sub")
        self.blk, self.sub = b, s
        self.core = lax.rem(b, 2)
        self.pos = [b // 4, lax.rem(b // 2, 2) * 2 + lax.rem(s, 2), s // 2]

    def at(self, pos, core):
        return ((pos[0] * 2 + pos[1] // 2) * 2 + core, pos[2] * 2 + lax.rem(pos[1], 2))

    def shift(self, axis, d):
        pos = list(self.pos)
        pos[axis] = lax.rem(pos[axis] + d, 4)
        return self.at(pos, self.core)

    def partition(self, d):
        return (lax.rem(self.blk + d, 16), self.sub)

    def sibling(self):
        return self.at(self.pos, 1 - self.core)


class Reduce:
    def __init__(self, place, n, off, g, full, rba, rbb, s1, rb2, s2, rb3, send_sems, recv_sems):
        self.p, self.n, self.off = place, n, off
        self.g, self.rba, self.rbb, self.s1, self.rb2, self.s2, self.rb3, self.full = g, rba, rbb, s1, rb2, s2, rb3, full
        self.send_sems, self.recv_sems = send_sems, recv_sems

    def put(self, step, part, src, dst, dev):
        pltpu.make_async_remote_copy(src_ref=src, dst_ref=dst, send_sem=self.send_sems.at[int(step == 8), part],
                                     recv_sem=self.recv_sems.at[step, part], device_id=dev,
                                     device_id_type=MESH).start()

    def got(self, step, part, tiles):
        ref = self.full.at[0, pl.ds(0, tiles)]
        pltpu.make_async_copy(ref, ref, self.recv_sems.at[step, part]).wait()

    def close(self):
        for part in range(3):
            for k, tiles in enumerate((33 * self.n, 16 * self.n)):
                ref = self.full.at[0, pl.ds(0, tiles)]
                pltpu.make_async_copy(ref, ref, self.send_sems.at[k, part]).wait()

    def axis(self, part, level):
        return (part + level) % 3

    def here(self, part, level):
        return self.p.pos[self.axis(part, level)]

    def half(self, part, c, k, level=0):
        return pl.ds(self.off + part * 16 * self.n + c * (4 * self.n) + k * (2 * self.n), 2 * self.n)

    def rs1(self, part):
        n, c, a = self.n, self.here(part, 0), self.axis(part, 0)
        for k, d in enumerate((1, 3)):
            self.put(0, part, self.g.at[self.half(part, lax.rem(c + 2, 4), k)], self.rba.at[part, k], self.p.shift(a, d))
        for k, d in enumerate((1, 3)):
            self.put(1, part, self.g.at[self.half(part, lax.rem(c + d, 4), 1 - k)],
                     self.rbb.at[part, k, pl.ds((1 - k) * 2 * n, 2 * n)], self.p.shift(a, d))

    def rs1_mid(self, part):
        n, c, a = self.n, self.here(part, 0), self.axis(part, 0)
        self.got(0, part, 4 * n)
        for k, d in enumerate((1, 3)):
            here = self.half(part, lax.rem(c + d, 4), k)
            self.g[here] = self.g[here] + self.rba[part, k]
            self.put(1, part, self.g.at[here], self.rbb.at[part, k, pl.ds(k * 2 * n, 2 * n)], self.p.shift(a, d))

    def rs1_done(self, part):
        n, c = self.n, self.here(part, 0)
        self.got(1, part, 8 * n)
        off = self.off + part * 16 * n + c * (4 * n)
        self.s1[part] = self.g[pl.ds(off, 4 * n)] + (self.rbb[part, 0] + self.rbb[part, 1])

    def rs2(self, part):
        n, c, a = self.n, self.here(part, 1), self.axis(part, 1)
        for d in (2, 1, 3):
            self.put(2, part, self.s1.at[part, pl.ds(lax.rem(c + d, 4) * n, n)], self.rb2.at[part, d - 1],
                     self.p.shift(a, d))

    def rs2_done(self, part):
        n, c = self.n, self.here(part, 1)
        self.got(2, part, 3 * n)
        self.s2[part] = (self.s1[part, pl.ds(c * n, n)] + self.rb2[part, 0]) + (self.rb2[part, 1] + self.rb2[part, 2])

    def ar3(self, part):
        c, a = self.here(part, 2), self.axis(part, 2)
        for d in (2, 1, 3):
            self.put(3, part, self.s2.at[part], self.rb3.at[part, c], self.p.shift(a, d))
        self.rb3[part, c] = self.s2[part]

    def mine(self, part):
        n = self.n
        return self.off + part * 16 * n + self.here(part, 0) * (4 * n) + self.here(part, 1) * n

    def ar3_done(self, part):
        self.got(3, part, 3 * self.n)
        self.full[self.p.core, pl.ds(self.mine(part), self.n)] = (
            (self.rb3[part, 0] + self.rb3[part, 1]) + (self.rb3[part, 2] + self.rb3[part, 3]))

    def ag2(self, part):
        a = self.axis(part, 1)
        ref = self.full.at[self.p.core, pl.ds(self.mine(part), self.n)]
        for d in (2, 1, 3):
            self.put(4, part, ref, ref, self.p.shift(a, d))

    def ag2_done(self, part):
        self.got(4, part, 3 * self.n)

    def chunk(self, part, c):
        return self.full.at[self.p.core, pl.ds(self.off + part * 16 * self.n + c * (4 * self.n), 4 * self.n)]

    def far(self, part, c, k):
        return self.full.at[self.p.core, self.half(part, c, k)]

    def ag1(self, part):
        c, a = self.here(part, 0), self.axis(part, 0)
        for j in range(2):
            for k, d in enumerate((1, 3)):
                ref = self.far(part, c, (k + j) % 2)
                self.put(5 + j, part, ref, ref, self.p.shift(a, d))
        ref = self.chunk(part, c)
        self.put(8, part, ref, ref, self.p.sibling())

    def ag1_mid(self, part):
        c, a = self.here(part, 0), self.axis(part, 0)
        self.got(5, part, 4 * self.n)
        for k, d in enumerate((1, 3)):
            ref = self.far(part, lax.rem(c + 4 - d, 4), k)
            self.put(7, part, ref, ref, self.p.shift(a, d))

    def ag1_near(self, part):
        c = self.here(part, 0)
        self.got(6, part, 4 * self.n)
        for k, d in enumerate((1, 3)):
            ref = self.chunk(part, lax.rem(c + 4 - d, 4))
            self.put(8, part, ref, ref, self.p.sibling())

    def ag1_done(self, part):
        c = self.here(part, 0)
        self.got(7, part, 4 * self.n)
        ref = self.chunk(part, lax.rem(c + 2, 4))
        self.put(8, part, ref, ref, self.p.sibling())

    def both(self, part):
        self.got(8, part, 16 * self.n)

    def each(self, *steps):
        for part in range(3):
            for step in steps:
                step(part)


def tiles_of(x):
    return [x[:, k : k + 128].reshape(x.shape[0] // 8, 8, 128) for k in range(0, x.shape[1], 128)]


def scatter_into(g_ref, at, grad2, col, base, width, add):
    hot = lanes_hot(col, base, width).astype(F32).astype(BF16)
    for j, t in enumerate(tiles_of(fold(mm(grad2, hot)))):
        n = t.shape[0]
        here = pl.ds(at + j * n, n)
        g_ref[here] = g_ref[here] + t if add else t


def buckets(w, left_ref, lstate_ref, right_ref, rstate_ref, rel_ref, relstate_ref, hub_ref, hstate_ref, heads_hbm, rels_hbm, tails_hbm,
            negs_hbm, hubs_hbm, left_out, right_out, hub_out, rel_out,
            left, lstate, right, rstate, rel, relstate, hub_t, hstate, heads, rels, tails, negs, hubs,
            r_buf, dut, dus, dro, drs, mout, min_, hg, hfull, rg, rfull, xsem, isem, osem, *batches):
    place = Place()
    log, loads = [], {}
    feats, rows = left.shape
    e = heads.shape[1]
    m = hubs.shape[1]
    for k, (name, src, dst) in enumerate((
            ("heads", heads_hbm, heads), ("rels", rels_hbm, rels), ("left", left_ref, left), ("rel", rel_ref, rel),
            ("right", right_ref, right), ("tails", tails_hbm, tails), ("negs", negs_hbm, negs),
            ("rstate", rstate_ref, rstate), ("lstate", lstate_ref, lstate), ("hubs", hubs_hbm, hubs),
            ("hub", hub_ref, hub_t), ("relstate", relstate_ref, relstate), ("hstate", hstate_ref, hstate))):
        loads[name] = pltpu.make_async_copy(src, dst, isem.at[k])
        if not name.startswith("hub"):
            loads[name].start()
    red = []
    for g, full, sizes in ((hg, hfull, HUB_PARTS), (rg, rfull, REL_PARTS)):
        off = 0
        for n in sizes:
            red.append(Reduce(place, n, off, g, full, *batches[8 * len(red) : 8 * len(red) + 8]))
            off += 48 * n
    ha, hb, rc = red
    barrier = pltpu.get_barrier_semaphore()
    for a in range(3):
        for d in (1, 2, 3):
            pl.semaphore_signal(barrier, inc=1, device_id=place.shift(a, d), device_id_type=MESH)
    for dev in (place.sibling(), place.partition(1), place.partition(15)):
        pl.semaphore_signal(barrier, inc=1, device_id=dev, device_id_type=MESH)

    def send(k, src, dst, dev):
        return Sent(src, dst, xsem.at[0, k], xsem.at[1, k], dev, log)

    for name in ("heads", "rels", "left", "rel"):
        loads[name].wait()
    loads["hub"].start()
    loads["hubs"].start()
    idx_r = jnp.concatenate([rels[0:1, :], rels[1:2, :]], axis=1)
    r_buf[...] = fold(mm(stacked(rel[...]), rows_hot(idx_r, 0, rel.shape[1])))
    h0 = fold(gather(left[...], heads[0:1, :]))
    q0 = cmul(h0, r_buf[:, :e])
    for name in ("right", "tails", "negs", "rstate"):
        loads[name].wait()
    q0t = stacked(q0.T)
    q02 = stacked(q0)
    r2 = stacked(right[...])
    coef = coefs(mm3(q0t, r2[:feats], r2[feats:]), w, tails[0:1, :], negs[0:1, :], rows)
    ch, cl = halves(coef)
    mout[:feats, :], state1 = adagrad(right[...], rstate[...], mm3(q02, ch, cl))
    mout[feats:, :] = jnp.broadcast_to(state1, (8, rows))
    pl.semaphore_wait(barrier, 12)
    x_m = send(3, mout, min_, place.partition(1))

    loads["hubs"].wait()
    loads["hub"].wait()
    idx_u = jnp.concatenate([hubs[0:1, :], hubs[1:2, :]], axis=1)
    u = mm(stacked(hub_t[...]), rows_hot(idx_u, 0, hub_t.shape[1])).astype(BF16)
    u0, u1 = u[:, :m], u[:, m:]
    ch2, cl2 = halves(sigmoid(mm3(q0t, u0[:feats], u0[feats:])) * w)
    dq = mm3(r2, ch, cl, NT) + mm3(u0, ch2, cl2, NT)
    dh = cmul_conj(dq, r_buf[:, :e])
    gl = fold(mm(stacked(dh), lanes_hot(column(heads[0:1, :]), 0, rows).astype(F32).astype(BF16)))
    loads["lstate"].wait()
    left[...], lstate[...] = adagrad(left[...], lstate[...], gl)
    dro[0, :feats, :] = cmul_conj(dq, h0)
    dro[0, feats:, :] = jnp.broadcast_to(rels[0:1, :].astype(F32), (8, e))
    x_r0 = send(1, dro.at[0], drs.at[0], place.sibling())
    h1 = fold(gather(left[...], heads[1:2, :]))
    q1 = cmul(h1, r_buf[:, e:])
    q1t = stacked(q1.T)
    q12 = stacked(q1)
    ch3, cl3 = halves(sigmoid(mm3(q1t, u1[:feats], u1[feats:])) * w)
    dut[:feats, :m] = mm3(q02, ch2, cl2)
    dut[:feats, m:] = mm3(q12, ch3, cl3)
    dut[feats:, :] = jnp.broadcast_to(idx_u.astype(F32), (8, 2 * m))
    x_u = send(0, dut, dus, place.sibling())

    half_lanes = hub_t.shape[1] // 2
    first_lane = place.core * half_lanes
    own2 = stacked(dut[:feats, :])
    own_col = column(idx_u)
    for k in range(4):
        scatter_into(hg, k * 200, own2, own_col, first_lane + k * 512, 512, False)
    hg[800:, :, :] = jnp.zeros((hg.shape[0] - 800, 8, 128), F32)
    x_u.wait_recv()
    sib2 = stacked(dus[:feats, :])
    sib_col = column(dus[feats : feats + 1, :].astype(jnp.int32))
    for k in range(4):
        scatter_into(hg, k * 200, sib2, sib_col, first_lane + k * 512, 512, True)
        if k == 2:
            ha.each(ha.rs1)
    hb.each(hb.rs1)
    dq1h = mm3(u1, ch3, cl3, NT)
    first_rel = place.core * (rel.shape[1] // 2)

    def rel_scatter(x, add):
        scatter_into(rg, 0, stacked(x[:feats, :]), column(x[feats : feats + 1, :].astype(jnp.int32)), first_rel, 640,
                     add)

    x_m.wait_recv()
    r2 = stacked(min_[:feats, :])
    coef = coefs(mm3(q1t, r2[:feats], r2[feats:]), w, tails[1:2, :], negs[1:2, :], rows)
    ha.each(ha.rs1_mid)
    ch, cl = halves(coef)
    dq = mm3(r2, ch, cl, NT) + dq1h
    dro[1, :feats, :] = cmul_conj(dq, h1)
    dro[1, feats:, :] = jnp.broadcast_to(rels[1:2, :].astype(F32), (8, e))
    x_r1 = send(2, dro.at[1], drs.at[1], place.sibling())
    hb.each(hb.rs1_mid)
    rel_scatter(dro[0], False)
    x_r0.wait_recv()
    rel_scatter(drs[0], True)
    rg[250:, :, :] = jnp.zeros((rg.shape[0] - 250, 8, 128), F32)
    rel_scatter(dro[1], True)
    x_r1.wait_recv()
    rel_scatter(drs[1], True)
    rc.each(rc.rs1)
    ha.each(ha.rs1_done, ha.rs2)
    g = mm3(q12, ch, cl)
    right_out[...], _ = adagrad(min_[:feats, :], min_[feats : feats + 1, :], g)
    rc.each(rc.rs1_mid)
    ha.each(ha.rs2_done, ha.ar3)
    hb.each(hb.rs1_done, hb.rs2)
    dh = cmul_conj(dq, r_buf[:, e:])
    gl = fold(mm(stacked(dh), lanes_hot(column(heads[1:2, :]), 0, rows).astype(F32).astype(BF16)))
    left_out[...], _ = adagrad(left[...], lstate[...], gl)
    ha.each(ha.ar3_done, ha.ag2)
    rc.each(rc.rs1_done, rc.rs2)
    hb.each(hb.rs2_done, hb.ar3)
    ha.each(ha.ag2_done, ha.ag1)
    rc.each(rc.rs2_done, rc.ar3)
    ha.each(ha.ag1_mid)
    hb.each(hb.ar3_done, hb.ag2)
    rc.each(rc.ar3_done, rc.ag2)
    hb.each(hb.ag2_done, hb.ag1)
    ha.each(ha.ag1_near)
    rc.each(rc.ag2_done, rc.ag1)
    hb.each(hb.ag1_mid)
    ha.each(ha.ag1_done)
    rc.each(rc.ag1_mid)
    hb.each(hb.ag1_near)
    loads["hstate"].wait()
    loads["relstate"].wait()
    outs = []

    def final(table, state, full, out, at, number, lanes):
        n = feats // 8
        count = lanes // 2 // 128
        for h in range(2):
            for j in range(at, at + number):
                here = slice((h * count + j) * 128, (h * count + j + 1) * 128)
                gj = full[h, j * n : (j + 1) * n].reshape(feats, 128)
                new = state[h * count + j : h * count + j + 1, :] + jnp.sum(gj * gj, axis=0, keepdims=True) * (1.0 / feats)
                table[:, here] = table[:, here] - gj * (RATE / jnp.sqrt(new))
            here = pl.ds((h * count + at) * 128, number * 128)
            outs.append(pltpu.make_async_copy(table.at[:, here], out.at[:, here], osem.at[len(outs)]))
            outs[-1].start()

    ha.each(ha.both)
    final(hub_t, hstate, hfull, hub_out, 0, 8, hub_t.shape[1])
    hb.each(hb.ag1_done)
    rc.each(rc.ag1_near)
    rc.each(rc.ag1_done)
    hb.each(hb.both)
    final(hub_t, hstate, hfull, hub_out, 8, 8, hub_t.shape[1])
    rc.each(rc.both)
    final(rel, relstate, rfull, rel_out, 0, 5, rel.shape[1])
    for c in log + red:
        c.close()
    for c in outs:
        c.wait()


def hand_on(*refs):
    n = (len(refs) - 1) // 3
    steps = []
    for src, dst, mid in zip(refs[:n], refs[n : 2 * n], refs[2 * n : 3 * n]):
        cut = src.shape[0] // 5
        for k in range(5):
            here = pl.ds(k * cut, cut)
            sem = refs[-1].at[len(steps)]
            steps.append((pltpu.make_async_copy(src.at[here], mid.at[here], sem),
                          pltpu.make_async_copy(mid.at[here], dst.at[here], sem)))
            steps[-1][0].start()
    for load, store in steps:
        load.wait()
        store.start()
    for load, store in steps:
        store.wait()


def shards(left_emb, left_state, right_emb, right_state, relation_emb, relation_state, hub_emb, hub_state, heads,
           relations, tails, negatives, hub_ids):
    two, half, rows = left_emb.shape
    feats = two * half
    e = heads.shape[1]
    m = hub_ids.shape[1]
    w = 1.0 / (negatives.shape[1] + hub_ids.shape[1])
    left = left_emb.reshape(feats, rows)
    right = right_emb.reshape(feats, rows)
    rel = relation_emb.reshape(feats, -1)
    hub = hub_emb.reshape(feats, -1)
    sd = lambda *s: jax.ShapeDtypeStruct(s, F32)
    vm = pl.BlockSpec(memory_space=pltpu.VMEM)
    hbm = pl.BlockSpec(memory_space=pl.ANY)
    tile = lambda *s: pltpu.VMEM((*s, 8, 128), F32)
    fl = lambda *s: pltpu.VMEM(s, F32)
    it = lambda *s: pltpu.VMEM(s, jnp.int32)
    dma = pltpu.SemaphoreType.DMA
    batch = lambda n: [tile(3, 2, 2 * n), tile(3, 2, 4 * n), tile(3, 4 * n), tile(3, 3, n), tile(3, n), tile(3, 4, n),
                       dma((2, 3)), dma((9, 3))]
    ht, rt = 48 * sum(HUB_PARTS), 48 * sum(REL_PARTS)
    outs = [sd(feats, rows), sd(feats, rows), sd(*hub.shape), sd(*rel.shape)]
    left2, right2, hub_new, rel_new = pl.pallas_call(
        functools.partial(buckets, w), out_shape=outs, in_specs=[hbm] * 13, out_specs=[vm, vm, hbm, hbm],
        scratch_shapes=[
            fl(feats, rows), fl(1, rows), fl(feats, rows), fl(1, rows), fl(feats, rel.shape[1]),
            fl(rel.shape[1] // 128, 128), fl(feats, hub.shape[1]), fl(hub.shape[1] // 128, 128),
            it(2, e), it(2, e), it(2, e), it(2, negatives.shape[1]), it(2, m),
            fl(feats, 2 * e), fl(feats + 8, 2 * m), fl(feats + 8, 2 * m), fl(2, feats + 8, e), fl(2, feats + 8, e),
            fl(feats + 8, rows), fl(feats + 8, rows), tile(ht), tile(2, ht), tile(rt), tile(2, rt),
            dma((2, 4)), dma((13,)), dma((6,)), *(x for n in HUB_PARTS + REL_PARTS for x in batch(n))],
        compiler_params=pltpu.CompilerParams(vmem_limit_bytes=VMEM_MIB * 2**20, collective_id=1, has_side_effects=True),
        name="buckets",
    )(left, left_state[None], right, right_state[None], rel, relation_state.reshape(-1, 128), hub,
      hub_state.reshape(-1, 128), heads, relations, tails, negatives, hub_ids)
    outs = [left2, right2, rel_new, hub_new]
    left2, right2, rel_new, hub_new = pl.pallas_call(
        hand_on, out_shape=[sd(*x.shape) for x in outs], in_specs=[hbm] * 4, out_specs=[hbm] * 4,
        scratch_shapes=[*(fl(*x.shape) for x in outs), dma((len(outs) * 5,))], name="hand_on",
        compiler_params=pltpu.CompilerParams(vmem_limit_bytes=60 * 2**20),
    )(*outs)
    return (left2.reshape(left_emb.shape), right2.reshape(right_emb.shape), rel_new.reshape(relation_emb.shape),
            hub_new.reshape(hub_emb.shape))


def solution(mesh):
    cut = P(None, None, ("blk", "sub"))
    row = P(("blk", "sub"))
    idx = P(None, ("blk", "sub"))
    return jax.shard_map(shards, mesh=mesh, in_specs=(cut, row, cut, row, P(), P(), P(), P(), idx, idx, idx, idx, idx),
                         out_specs=(cut, cut, P(), P()), check_vma=False)
```

time: 246 us -> 89.6 us (0.36)
  waiting for transfers between devices: 175 us -> 0 us
  Pallas kernels: 40.8 us -> 88.7 us
  between operations: 14.1 us -> 0.8 us
  other arithmetic: 10.5 us -> 0 us
  starting transfers between devices: 4.59 us -> 0 us
    psum x1 -> x0, waiting for transfers between devices: 165 us -> none  [shards(): grel, ghub = lax.psum((grel, ghub), ('blk', 'sub'))]
    pallas_call x2, Pallas kernels: 40.8 us -> 88.7 us  [the longest x1 80.5 us: shards(): pl.pallas_call(functools.partial(buckets, w), out_shape=outs, in_specs=[h...]
    ppermute x2 -> x0, waiting for transfers between devices: 9.35 us -> none  [shards(): lax.ppermute((right1, rs1), 'blk', [(i, (i + 1) % n) for i in range(n)])]
    sub x2 -> x0, other arithmetic: 7.9 us -> none  [step(): return table - RATE * grads / jnp.sqrt(new)[None, :]]
    ppermute x2 -> x0, starting transfers between devices: 4.55 us -> none  [shards(): lax.ppermute((right1, rs1), 'blk', [(i, (i + 1) % n) for i in range(n)])]
    reduce_sum x2 -> x0, other arithmetic: 2.57 us -> none  [step(): new = state + jnp.mean(grads * grads, axis=0)]
  transfers between devices with their start and end apart: 3 -> 0, of which waited for: 2 -> 0; matrix products, arithmetic and copies ran while one was open for 0% -> 0% of each run, Pallas kernels for 0% -> 0%
where the time goes in v2:
time: 89.6 us; the launch traced here: 89.5 us
  Pallas kernels  88.7 us (99%)
    pallas_call x1, Pallas kernels, shards(): pl.pallas_call(functools.partial(buckets, w), out_shape=outs, in_specs=[h...  80.5 us
    pallas_call x1, Pallas kernels, shards(): pl.pallas_call(hand_on, out_shape=[sd(*x.shape) for x in outs], in_specs=...  8.19 us

profile of v2, /device:TPU:1, one launch (start us, length us, event | category | flops | bytes accessed | tf_op | source)
XLA Modules:
  0.0 89.5 jit_solution(8218939934014706528)
XLA Ops:
  0.6 80.5 %buckets.1 = (f32[400,512]{1,0:T(8,128)}, f32[400,512]{1,0:T(8,128)}, f32[400,4096]{1,0:T(8,128)}, f32[400,1280]{1,0:T(8,128)}) custom-call(f32[400,512]{1,0:T(8,128)} %bitcast.14, f32[1,512]{1,0:T(1,128)} %bitcast.18, f32[400,512]{1,0:T(8,128)} %bitcast.15, f32[1,512]{1,0:T(1,128)} %bitcast.19, f32[400,1280]{1,0:T(8,128)} %bitcast.13, f32[10,128]{1,0:T(8,128)} %bitcast.17, ...), custom_call_target="tpu_custom_call" | custom-call | tf_op jit(solution)/shard_map/buckets/pallas_call | solution.py:512
  81.1 8.2 %hand_on.1 = (f32[400,512]{1,0:T(8,128)}, f32[400,512]{1,0:T(8,128)}, f32[400,1280]{1,0:T(8,128)}, f32[400,4096]{1,0:T(8,128)}) custom-call(f32[400,512]{1,0:T(8,128)} %get-tuple-element.12.refs_0_, f32[400,512]{1,0:T(8,128)} %get-tuple-element.13.refs_1_, f32[400,1280]{1,0:T(8,128)} %get-tuple-element.14.refs_2_, f32[400,4096]{1,0:T(8,128)} %get-tuple-element.15.refs_3_), custom_call_target="tpu_custom_call" | custom-call | tf_op jit(solution)/shard_map/hand_on/pallas_call | solution.py:526

commit v3 on v2

--- a/solution.py
+++ b/solution.py
@@ -108,7 +108,7 @@
 
 
 VMEM_MIB = 54
-HUB_PARTS, REL_PARTS = (9, 8), (6,)
+PARTS = (8, 8, 6)
 MESH = pl.DeviceIdType.MESH
 
 
@@ -296,28 +296,28 @@
 
 
 def buckets(w, left_ref, lstate_ref, right_ref, rstate_ref, rel_ref, relstate_ref, hub_ref, hstate_ref, heads_hbm, rels_hbm, tails_hbm,
-            negs_hbm, hubs_hbm, left_out, right_out, hub_out, rel_out,
-            left, lstate, right, rstate, rel, relstate, hub_t, hstate, heads, rels, tails, negs, hubs,
-            r_buf, dut, dus, dro, drs, mout, min_, hg, hfull, rg, rfull, xsem, isem, osem, *batches):
+            negs_hbm, hubs_hbm, left_out, right_out, hub_t, rel,
+            left, lstate, right, rstate, relstate, hstate, heads, rels, tails, negs, hubs,
+            r_buf, dut, dus, dro, drs, mout, min_, g, full, xsem, isem, *batches):
     place = Place()
     log, loads = [], {}
     feats, rows = left.shape
     e = heads.shape[1]
     m = hubs.shape[1]
     for k, (name, src, dst) in enumerate((
-            ("heads", heads_hbm, heads), ("rels", rels_hbm, rels), ("left", left_ref, left), ("rel", rel_ref, rel),
+            ("rels", rels_hbm, rels), ("heads", heads_hbm, heads), ("rel", rel_ref, rel), ("left", left_ref, left),
             ("right", right_ref, right), ("tails", tails_hbm, tails), ("negs", negs_hbm, negs),
             ("rstate", rstate_ref, rstate), ("lstate", lstate_ref, lstate), ("hubs", hubs_hbm, hubs),
             ("hub", hub_ref, hub_t), ("relstate", relstate_ref, relstate), ("hstate", hstate_ref, hstate))):
         loads[name] = pltpu.make_async_copy(src, dst, isem.at[k])
         if not name.startswith("hub"):
             loads[name].start()
-    red = []
-    for g, full, sizes in ((hg, hfull, HUB_PARTS), (rg, rfull, REL_PARTS)):
-        off = 0
-        for n in sizes:
-            red.append(Reduce(place, n, off, g, full, *batches[8 * len(red) : 8 * len(red) + 8]))
-            off += 48 * n
+    hub_tiles = feats // 8 * (hub_t.shape[1] // 256)
+    rel_tiles = feats // 8 * (rel.shape[1] // 256)
+    red, off = [], 0
+    for n in PARTS:
+        red.append(Reduce(place, n, off, g, full, *batches[8 * len(red) : 8 * len(red) + 8]))
+        off += 48 * n
     ha, hb, rc = red
     barrier = pltpu.get_barrier_semaphore()
     for a in range(3):
@@ -378,21 +378,21 @@
     own2 = stacked(dut[:feats, :])
     own_col = column(idx_u)
     for k in range(4):
-        scatter_into(hg, k * 200, own2, own_col, first_lane + k * 512, 512, False)
-    hg[800:, :, :] = jnp.zeros((hg.shape[0] - 800, 8, 128), F32)
+        scatter_into(g, k * 200, own2, own_col, first_lane + k * 512, 512, False)
+    g[hub_tiles + rel_tiles :] = jnp.zeros((g.shape[0] - hub_tiles - rel_tiles, 8, 128), F32)
     x_u.wait_recv()
     sib2 = stacked(dus[:feats, :])
     sib_col = column(dus[feats : feats + 1, :].astype(jnp.int32))
     for k in range(4):
-        scatter_into(hg, k * 200, sib2, sib_col, first_lane + k * 512, 512, True)
-        if k == 2:
+        scatter_into(g, k * 200, sib2, sib_col, first_lane + k * 512, 512, True)
+        if k == 1:
             ha.each(ha.rs1)
     hb.each(hb.rs1)
     dq1h = mm3(u1, ch3, cl3, NT)
     first_rel = place.core * (rel.shape[1] // 2)
 
     def rel_scatter(x, add):
-        scatter_into(rg, 0, stacked(x[:feats, :]), column(x[feats : feats + 1, :].astype(jnp.int32)), first_rel, 640,
+        scatter_into(g, hub_tiles, stacked(x[:feats, :]), column(x[feats : feats + 1, :].astype(jnp.int32)), first_rel, 640,
                      add)
 
     x_m.wait_recv()
@@ -408,83 +408,71 @@
     rel_scatter(dro[0], False)
     x_r0.wait_recv()
     rel_scatter(drs[0], True)
-    rg[250:, :, :] = jnp.zeros((rg.shape[0] - 250, 8, 128), F32)
     rel_scatter(dro[1], True)
     x_r1.wait_recv()
     rel_scatter(drs[1], True)
     rc.each(rc.rs1)
     ha.each(ha.rs1_done, ha.rs2)
-    g = mm3(q12, ch, cl)
-    right_out[...], _ = adagrad(min_[:feats, :], min_[feats : feats + 1, :], g)
+    right_out[...], _ = adagrad(min_[:feats, :], min_[feats : feats + 1, :], mm3(q12, ch, cl))
+    hb.each(hb.rs1_done, hb.rs2)
     rc.each(rc.rs1_mid)
     ha.each(ha.rs2_done, ha.ar3)
-    hb.each(hb.rs1_done, hb.rs2)
     dh = cmul_conj(dq, r_buf[:, e:])
     gl = fold(mm(stacked(dh), lanes_hot(column(heads[1:2, :]), 0, rows).astype(F32).astype(BF16)))
     left_out[...], _ = adagrad(left[...], lstate[...], gl)
+    hb.each(hb.rs2_done, hb.ar3)
+    rc.each(rc.rs1_done, rc.rs2)
     ha.each(ha.ar3_done, ha.ag2)
-    rc.each(rc.rs1_done, rc.rs2)
-    hb.each(hb.rs2_done, hb.ar3)
+    hb.each(hb.ar3_done, hb.ag2)
+    rc.each(rc.rs2_done, rc.ar3)
     ha.each(ha.ag2_done, ha.ag1)
-    rc.each(rc.rs2_done, rc.ar3)
+    hb.each(hb.ag2_done, hb.ag1)
+    rc.each(rc.ar3_done, rc.ag2)
     ha.each(ha.ag1_mid)
-    hb.each(hb.ar3_done, hb.ag2)
-    rc.each(rc.ar3_done, rc.ag2)
-    hb.each(hb.ag2_done, hb.ag1)
+    hb.each(hb.ag1_mid)
+    rc.each(rc.ag2_done, rc.ag1)
     ha.each(ha.ag1_near)
-    rc.each(rc.ag2_done, rc.ag1)
-    hb.each(hb.ag1_mid)
+    hb.each(hb.ag1_near)
+    rc.each(rc.ag1_mid)
     ha.each(ha.ag1_done)
-    rc.each(rc.ag1_mid)
-    hb.each(hb.ag1_near)
     loads["hstate"].wait()
     loads["relstate"].wait()
-    outs = []
-
-    def final(table, state, full, out, at, number, lanes):
+
+    def final(table, state, first_tile, at, number, lanes):
         n = feats // 8
         count = lanes // 2 // 128
         for h in range(2):
             for j in range(at, at + number):
                 here = slice((h * count + j) * 128, (h * count + j + 1) * 128)
-                gj = full[h, j * n : (j + 1) * n].reshape(feats, 128)
+                gj = full[h, first_tile + j * n : first_tile + (j + 1) * n].reshape(feats, 128)
                 new = state[h * count + j : h * count + j + 1, :] + jnp.sum(gj * gj, axis=0, keepdims=True) * (1.0 / feats)
                 table[:, here] = table[:, here] - gj * (RATE / jnp.sqrt(new))
-            here = pl.ds((h * count + at) * 128, number * 128)
-            outs.append(pltpu.make_async_copy(table.at[:, here], out.at[:, here], osem.at[len(outs)]))
-            outs[-1].start()
 
     ha.each(ha.both)
-    final(hub_t, hstate, hfull, hub_out, 0, 8, hub_t.shape[1])
+    final(hub_t, hstate, 0, 0, 7, hub_t.shape[1])
     hb.each(hb.ag1_done)
     rc.each(rc.ag1_near)
     rc.each(rc.ag1_done)
     hb.each(hb.both)
-    final(hub_t, hstate, hfull, hub_out, 8, 8, hub_t.shape[1])
+    final(hub_t, hstate, 0, 7, 8, hub_t.shape[1])
     rc.each(rc.both)
-    final(rel, relstate, rfull, rel_out, 0, 5, rel.shape[1])
+    final(hub_t, hstate, 0, 15, 1, hub_t.shape[1])
+    final(rel, relstate, hub_tiles, 0, 5, rel.shape[1])
     for c in log + red:
         c.close()
-    for c in outs:
-        c.wait()
 
 
 def hand_on(*refs):
-    n = (len(refs) - 1) // 3
-    steps = []
-    for src, dst, mid in zip(refs[:n], refs[n : 2 * n], refs[2 * n : 3 * n]):
+    n = (len(refs) - 1) // 2
+    copies = []
+    for src, dst in zip(refs[:n], refs[n : 2 * n]):
         cut = src.shape[0] // 5
         for k in range(5):
             here = pl.ds(k * cut, cut)
-            sem = refs[-1].at[len(steps)]
-            steps.append((pltpu.make_async_copy(src.at[here], mid.at[here], sem),
-                          pltpu.make_async_copy(mid.at[here], dst.at[here], sem)))
-            steps[-1][0].start()
-    for load, store in steps:
-        load.wait()
-        store.start()
-    for load, store in steps:
-        store.wait()
+            copies.append(pltpu.make_async_copy(src.at[here], dst.at[here], refs[-1].at[len(copies)]))
+            copies[-1].start()
+    for c in copies:
+        c.wait()
 
 
 def shards(left_emb, left_state, right_emb, right_state, relation_emb, relation_state, hub_emb, hub_state, heads,
@@ -507,27 +495,27 @@
     dma = pltpu.SemaphoreType.DMA
     batch = lambda n: [tile(3, 2, 2 * n), tile(3, 2, 4 * n), tile(3, 4 * n), tile(3, 3, n), tile(3, n), tile(3, 4, n),
                        dma((2, 3)), dma((9, 3))]
-    ht, rt = 48 * sum(HUB_PARTS), 48 * sum(REL_PARTS)
-    outs = [sd(feats, rows), sd(feats, rows), sd(*hub.shape), sd(*rel.shape)]
+    total = 48 * sum(PARTS)
+    outs = [fl(feats, rows), fl(feats, rows), fl(*hub.shape), fl(*rel.shape)]
     left2, right2, hub_new, rel_new = pl.pallas_call(
-        functools.partial(buckets, w), out_shape=outs, in_specs=[hbm] * 13, out_specs=[vm, vm, hbm, hbm],
+        functools.partial(buckets, w), out_shape=outs, in_specs=[hbm] * 13, out_specs=[vm] * 4,
         scratch_shapes=[
-            fl(feats, rows), fl(1, rows), fl(feats, rows), fl(1, rows), fl(feats, rel.shape[1]),
-            fl(rel.shape[1] // 128, 128), fl(feats, hub.shape[1]), fl(hub.shape[1] // 128, 128),
+            fl(feats, rows), fl(1, rows), fl(feats, rows), fl(1, rows),
+            fl(rel.shape[1] // 128, 128), fl(hub.shape[1] // 128, 128),
             it(2, e), it(2, e), it(2, e), it(2, negatives.shape[1]), it(2, m),
             fl(feats, 2 * e), fl(feats + 8, 2 * m), fl(feats + 8, 2 * m), fl(2, feats + 8, e), fl(2, feats + 8, e),
-            fl(feats + 8, rows), fl(feats + 8, rows), tile(ht), tile(2, ht), tile(rt), tile(2, rt),
-            dma((2, 4)), dma((13,)), dma((6,)), *(x for n in HUB_PARTS + REL_PARTS for x in batch(n))],
+            fl(feats + 8, rows), fl(feats + 8, rows), tile(total), tile(2, total),
+            dma((2, 4)), dma((13,)), *(x for n in PARTS for x in batch(n))],
         compiler_params=pltpu.CompilerParams(vmem_limit_bytes=VMEM_MIB * 2**20, collective_id=1, has_side_effects=True),
         name="buckets",
     )(left, left_state[None], right, right_state[None], rel, relation_state.reshape(-1, 128), hub,
       hub_state.reshape(-1, 128), heads, relations, tails, negatives, hub_ids)
     outs = [left2, right2, rel_new, hub_new]
     left2, right2, rel_new, hub_new = pl.pallas_call(
-        hand_on, out_shape=[sd(*x.shape) for x in outs], in_specs=[hbm] * 4, out_specs=[hbm] * 4,
-        scratch_shapes=[*(fl(*x.shape) for x in outs), dma((len(outs) * 5,))], name="hand_on",
-        compiler_params=pltpu.CompilerParams(vmem_limit_bytes=60 * 2**20),
-    )(*outs)
+        hand_on, out_shape=[sd(*x.shape) for x in outs], in_specs=[vm] * 4, out_specs=[hbm] * 4,
+        scratch_shapes=[dma((len(outs) * 5,))], name="hand_on",
+        compiler_params=pltpu.CompilerParams(vmem_limit_bytes=4 * 2**20),
+    )(*(pltpu.with_memory_space_constraint(x, pltpu.VMEM) for x in outs))
     return (left2.reshape(left_emb.shape), right2.reshape(right_emb.shape), rel_new.reshape(relation_emb.shape),
             hub_new.reshape(hub_emb.shape))
 

time: 89.6 us -> 79.5 us (0.89)
  Pallas kernels: 88.7 us -> 78.6 us
    pallas_call x1, Pallas kernels: 80.5 us -> 74.6 us  [shards(): pl.pallas_call(functools.partial(buckets, w), out_shape=outs, in_specs=[h...]
    pallas_call x1, Pallas kernels: 8.19 us -> 4.06 us  [shards(): pl.pallas_call(hand_on, out_shape=[sd(*x.shape) for x in outs], in_specs=...]
where the time goes in v3:
time: 79.5 us; the launch traced here: 79.4 us
  Pallas kernels  78.6 us (99%)
  between operations  0.8 us (1%)
    pallas_call x1, Pallas kernels, shards(): pl.pallas_call(functools.partial(buckets, w), out_shape=outs, in_specs=[h...  74.6 us
    pallas_call x1, Pallas kernels, shards(): pl.pallas_call(hand_on, out_shape=[sd(*x.shape) for x in outs], in_specs=...  4.06 us

profile of v3, /device:TPU:1, one launch (start us, length us, event | category | flops | bytes accessed | tf_op | source)
XLA Modules:
  0.0 79.4 jit_solution(10017199860688642171)
XLA Ops:
  0.6 74.6 %buckets.1 = (f32[400,512]{1,0:T(8,128)S(1)}, f32[400,512]{1,0:T(8,128)S(1)}, f32[400,4096]{1,0:T(8,128)S(1)}, f32[400,1280]{1,0:T(8,128)S(1)}) custom-call(f32[400,512]{1,0:T(8,128)} %bitcast.14, f32[1,512]{1,0:T(1,128)} %bitcast.18, f32[400,512]{1,0:T(8,128)} %bitcast.15, f32[1,512]{1,0:T(1,128)} %bitcast.19, f32[400,1280]{1,0:T(8,128)} %bitcast.13, ...), custom_call_target="tpu_custom_call" | custom-call | tf_op jit(solution)/shard_map/buckets/pallas_call | solution.py:500
  75.2 4.1 %hand_on.1 = (f32[400,512]{1,0:T(8,128)}, f32[400,512]{1,0:T(8,128)}, f32[400,1280]{1,0:T(8,128)}, f32[400,4096]{1,0:T(8,128)}) custom-call(f32[400,512]{1,0:T(8,128)S(1)} %get-tuple-element.12.refs_0_, f32[400,512]{1,0:T(8,128)S(1)} %get-tuple-element.13.refs_1_, f32[400,1280]{1,0:T(8,128)S(1)} %get-tuple-element.14.refs_2_, ...), custom_call_target="tpu_custom_call" | custom-call | tf_op jit(solution)/shard_map/hand_on/pallas_call | solution.py:514

commit v4 on v3

--- a/solution.py
+++ b/solution.py
@@ -360,9 +360,6 @@
     gl = fold(mm(stacked(dh), lanes_hot(column(heads[0:1, :]), 0, rows).astype(F32).astype(BF16)))
     loads["lstate"].wait()
     left[...], lstate[...] = adagrad(left[...], lstate[...], gl)
-    dro[0, :feats, :] = cmul_conj(dq, h0)
-    dro[0, feats:, :] = jnp.broadcast_to(rels[0:1, :].astype(F32), (8, e))
-    x_r0 = send(1, dro.at[0], drs.at[0], place.sibling())
     h1 = fold(gather(left[...], heads[1:2, :]))
     q1 = cmul(h1, r_buf[:, e:])
     q1t = stacked(q1.T)
@@ -372,6 +369,10 @@
     dut[:feats, m:] = mm3(q12, ch3, cl3)
     dut[feats:, :] = jnp.broadcast_to(idx_u.astype(F32), (8, 2 * m))
     x_u = send(0, dut, dus, place.sibling())
+
+    dro[0, :feats, :] = cmul_conj(dq, h0)
+    dro[0, feats:, :] = jnp.broadcast_to(rels[0:1, :].astype(F32), (8, e))
+    x_r0 = send(1, dro.at[0], drs.at[0], place.sibling())
 
     half_lanes = hub_t.shape[1] // 2
     first_lane = place.core * half_lanes
@@ -388,6 +389,7 @@
         if k == 1:
             ha.each(ha.rs1)
     hb.each(hb.rs1)
+
     dq1h = mm3(u1, ch3, cl3, NT)
     first_rel = place.core * (rel.shape[1] // 2)
 
@@ -395,46 +397,48 @@
         scatter_into(g, hub_tiles, stacked(x[:feats, :]), column(x[feats : feats + 1, :].astype(jnp.int32)), first_rel, 640,
                      add)
 
+    rel_scatter(dro[0], False)
+    x_r0.wait_recv()
+    rel_scatter(drs[0], True)
     x_m.wait_recv()
     r2 = stacked(min_[:feats, :])
-    coef = coefs(mm3(q1t, r2[:feats], r2[feats:]), w, tails[1:2, :], negs[1:2, :], rows)
+    score = mm3(q1t, r2[:feats], r2[feats:])
     ha.each(ha.rs1_mid)
-    ch, cl = halves(coef)
+    ch, cl = halves(coefs(score, w, tails[1:2, :], negs[1:2, :], rows))
     dq = mm3(r2, ch, cl, NT) + dq1h
     dro[1, :feats, :] = cmul_conj(dq, h1)
     dro[1, feats:, :] = jnp.broadcast_to(rels[1:2, :].astype(F32), (8, e))
     x_r1 = send(2, dro.at[1], drs.at[1], place.sibling())
     hb.each(hb.rs1_mid)
-    rel_scatter(dro[0], False)
-    x_r0.wait_recv()
-    rel_scatter(drs[0], True)
     rel_scatter(dro[1], True)
     x_r1.wait_recv()
     rel_scatter(drs[1], True)
     rc.each(rc.rs1)
+    right_out[...], _ = adagrad(min_[:feats, :], min_[feats : feats + 1, :], mm3(q12, ch, cl))
     ha.each(ha.rs1_done, ha.rs2)
-    right_out[...], _ = adagrad(min_[:feats, :], min_[feats : feats + 1, :], mm3(q12, ch, cl))
+    rc.each(rc.rs1_mid)
     hb.each(hb.rs1_done, hb.rs2)
-    rc.each(rc.rs1_mid)
     ha.each(ha.rs2_done, ha.ar3)
+    rc.each(rc.rs1_done, rc.rs2)
+    hb.each(hb.rs2_done, hb.ar3)
+    ha.each(ha.ar3_done, ha.ag2)
+    rc.each(rc.rs2_done, rc.ar3)
+    hb.each(hb.ar3_done, hb.ag2)
+    ha.each(ha.ag2_done, ha.ag1)
+    rc.each(rc.ar3_done, rc.ag2)
+    hb.each(hb.ag2_done, hb.ag1)
     dh = cmul_conj(dq, r_buf[:, e:])
     gl = fold(mm(stacked(dh), lanes_hot(column(heads[1:2, :]), 0, rows).astype(F32).astype(BF16)))
     left_out[...], _ = adagrad(left[...], lstate[...], gl)
-    hb.each(hb.rs2_done, hb.ar3)
-    rc.each(rc.rs1_done, rc.rs2)
-    ha.each(ha.ar3_done, ha.ag2)
-    hb.each(hb.ar3_done, hb.ag2)
-    rc.each(rc.rs2_done, rc.ar3)
-    ha.each(ha.ag2_done, ha.ag1)
-    hb.each(hb.ag2_done, hb.ag1)
-    rc.each(rc.ar3_done, rc.ag2)
     ha.each(ha.ag1_mid)
-    hb.each(hb.ag1_mid)
     rc.each(rc.ag2_done, rc.ag1)
     ha.each(ha.ag1_near)
+    hb.each(hb.ag1_mid)
+    rc.each(rc.ag1_mid)
     hb.each(hb.ag1_near)
-    rc.each(rc.ag1_mid)
     ha.each(ha.ag1_done)
+    rc.each(rc.ag1_near)
+    hb.each(hb.ag1_done)
     loads["hstate"].wait()
     loads["relstate"].wait()
 
@@ -450,8 +454,6 @@
 
     ha.each(ha.both)
     final(hub_t, hstate, 0, 0, 7, hub_t.shape[1])
-    hb.each(hb.ag1_done)
-    rc.each(rc.ag1_near)
     rc.each(rc.ag1_done)
     hb.each(hb.both)
     final(hub_t, hstate, 0, 7, 8, hub_t.shape[1])

time: 79.5 us -> 75.5 us (0.950)
  Pallas kernels: 78.6 us -> 74.5 us
    pallas_call x1, Pallas kernels: 74.6 us -> 70.5 us  [shards(): pl.pallas_call(functools.partial(buckets, w), out_shape=outs, in_specs=[h...]
where the time goes in v4:
time: 75.5 us; the launch traced here: 75.3 us
  Pallas kernels  74.5 us (99%)
  between operations  0.8 us (1%)
    pallas_call x1, Pallas kernels, shards(): pl.pallas_call(functools.partial(buckets, w), out_shape=outs, in_specs=[h...  70.5 us
    pallas_call x1, Pallas kernels, shards(): pl.pallas_call(hand_on, out_shape=[sd(*x.shape) for x in outs], in_specs=...  4.06 us

profile of v4, /device:TPU:1, one launch (start us, length us, event | category | flops | bytes accessed | tf_op | source)
XLA Modules:
  0.0 75.3 jit_solution(18370081794578313429)
XLA Ops:
  0.6 70.5 %buckets.1 = (f32[400,512]{1,0:T(8,128)S(1)}, f32[400,512]{1,0:T(8,128)S(1)}, f32[400,4096]{1,0:T(8,128)S(1)}, f32[400,1280]{1,0:T(8,128)S(1)}) custom-call(f32[400,512]{1,0:T(8,128)} %bitcast.14, f32[1,512]{1,0:T(1,128)} %bitcast.18, f32[400,512]{1,0:T(8,128)} %bitcast.15, f32[1,512]{1,0:T(1,128)} %bitcast.19, f32[400,1280]{1,0:T(8,128)} %bitcast.13, ...), custom_call_target="tpu_custom_call" | custom-call | tf_op jit(solution)/shard_map/buckets/pallas_call | solution.py:502
  71.1 4.1 %hand_on.1 = (f32[400,512]{1,0:T(8,128)}, f32[400,512]{1,0:T(8,128)}, f32[400,1280]{1,0:T(8,128)}, f32[400,4096]{1,0:T(8,128)}) custom-call(f32[400,512]{1,0:T(8,128)S(1)} %get-tuple-element.12.refs_0_, f32[400,512]{1,0:T(8,128)S(1)} %get-tuple-element.13.refs_1_, f32[400,1280]{1,0:T(8,128)S(1)} %get-tuple-element.14.refs_2_, ...), custom_call_target="tpu_custom_call" | custom-call | tf_op jit(solution)/shard_map/hand_on/pallas_call | solution.py:516

commit v5 on v4

--- a/solution.py
+++ b/solution.py
@@ -153,7 +153,8 @@
 
 
 class Reduce:
-    def __init__(self, place, n, off, g, full, rba, rbb, s1, rb2, s2, rb3, send_sems, recv_sems):
+    def __init__(self, direct, place, n, off, g, full, rba, rbb, s1, rb2, s2, rb3, send_sems, recv_sems):
+        self.direct = direct
         self.p, self.n, self.off = place, n, off
         self.g, self.rba, self.rbb, self.s1, self.rb2, self.s2, self.rb3, self.full = g, rba, rbb, s1, rb2, s2, rb3, full
         self.send_sems, self.recv_sems = send_sems, recv_sems
@@ -247,6 +248,12 @@
 
     def ag1(self, part):
         c, a = self.here(part, 0), self.axis(part, 0)
+        if self.direct:
+            ref = self.chunk(part, c)
+            for d in (2, 1, 3):
+                self.put(5, part, ref, ref, self.p.shift(a, d))
+            self.put(8, part, ref, ref, self.p.sibling())
+            return
         for j in range(2):
             for k, d in enumerate((1, 3)):
                 ref = self.far(part, c, (k + j) % 2)
@@ -270,6 +277,12 @@
 
     def ag1_done(self, part):
         c = self.here(part, 0)
+        if self.direct:
+            self.got(5, part, 12 * self.n)
+            for d in (1, 2, 3):
+                ref = self.chunk(part, lax.rem(c + d, 4))
+                self.put(8, part, ref, ref, self.p.sibling())
+            return
         self.got(7, part, 4 * self.n)
         ref = self.chunk(part, lax.rem(c + 2, 4))
         self.put(8, part, ref, ref, self.p.sibling())
@@ -316,7 +329,7 @@
     rel_tiles = feats // 8 * (rel.shape[1] // 256)
     red, off = [], 0
     for n in PARTS:
-        red.append(Reduce(place, n, off, g, full, *batches[8 * len(red) : 8 * len(red) + 8]))
+        red.append(Reduce(len(red) == 2, place, n, off, g, full, *batches[8 * len(red) : 8 * len(red) + 8]))
         off += 48 * n
     ha, hb, rc = red
     barrier = pltpu.get_barrier_semaphore()
@@ -434,10 +447,8 @@
     rc.each(rc.ag2_done, rc.ag1)
     ha.each(ha.ag1_near)
     hb.each(hb.ag1_mid)
-    rc.each(rc.ag1_mid)
     hb.each(hb.ag1_near)
     ha.each(ha.ag1_done)
-    rc.each(rc.ag1_near)
     hb.each(hb.ag1_done)
     loads["hstate"].wait()
     loads["relstate"].wait()

time: 75.5 us -> 76.7 us (1.016)
  Pallas kernels: 74.5 us -> 75.8 us
    pallas_call x1, Pallas kernels: 70.5 us -> 71.7 us  [shards(): pl.pallas_call(functools.partial(buckets, w), out_shape=outs, in_specs=[h...]
where the time goes in v5:
time: 76.7 us; the launch traced here: 76.6 us
  Pallas kernels  75.8 us (99%)
  between operations  0.8 us (1%)
    pallas_call x1, Pallas kernels, shards(): pl.pallas_call(functools.partial(buckets, w), out_shape=outs, in_specs=[h...  71.7 us
    pallas_call x1, Pallas kernels, shards(): pl.pallas_call(hand_on, out_shape=[sd(*x.shape) for x in outs], in_specs=...  4.06 us

profile of v5, /device:TPU:1, one launch (start us, length us, event | category | flops | bytes accessed | tf_op | source)
XLA Modules:
  0.0 76.6 jit_solution(5690189422655842334)
XLA Ops:
  0.6 71.7 %buckets.1 = (f32[400,512]{1,0:T(8,128)S(1)}, f32[400,512]{1,0:T(8,128)S(1)}, f32[400,4096]{1,0:T(8,128)S(1)}, f32[400,1280]{1,0:T(8,128)S(1)}) custom-call(f32[400,512]{1,0:T(8,128)} %bitcast.14, f32[1,512]{1,0:T(1,128)} %bitcast.18, f32[400,512]{1,0:T(8,128)} %bitcast.15, f32[1,512]{1,0:T(1,128)} %bitcast.19, f32[400,1280]{1,0:T(8,128)} %bitcast.13, ...), custom_call_target="tpu_custom_call" | custom-call | tf_op jit(solution)/shard_map/buckets/pallas_call | solution.py:513
  72.4 4.1 %hand_on.1 = (f32[400,512]{1,0:T(8,128)}, f32[400,512]{1,0:T(8,128)}, f32[400,1280]{1,0:T(8,128)}, f32[400,4096]{1,0:T(8,128)}) custom-call(f32[400,512]{1,0:T(8,128)S(1)} %get-tuple-element.12.refs_0_, f32[400,512]{1,0:T(8,128)S(1)} %get-tuple-element.13.refs_1_, f32[400,1280]{1,0:T(8,128)S(1)} %get-tuple-element.14.refs_2_, ...), custom_call_target="tpu_custom_call" | custom-call | tf_op jit(solution)/shard_map/hand_on/pallas_call | solution.py:527
